TPU v7x, 512 devices: a whole 4x4x16 slice. The times are simulated.
512 devices in a mesh: dp: 32 (over x, z_lo, core), mp: 16 (over y, z_hi).
Axes of the slice: x: 4, y: 4, z: 16 (z_hi: 4, z_lo: 4; z = z_hi * 4 + z_lo), core: 2. Of those that a mesh axis runs over, the one named last changes fastest.
Arguments:
- reference_hidden_states: bfloat16 [512, 32, 8, 3072], P('dp', 'mp'), may hold values from -700 to 700
- policy_hidden_states: bfloat16 [512, 32, 8, 3072], P(('dp', 'mp')), may hold values from -700 to 700
- reference_norm_gain: float32 [3072], replicated, may hold values from 0.5 to 1.5
- policy_norm_gain: float32 [3072], replicated, may hold values from 0.5 to 1.5
- action_head_weight: bfloat16 [3072, 2048], P('mp'), may hold values from -0.3125 to 0.3125
- adapter_down_weight: bfloat16 [3072, 64], P('mp'), may hold values from -0.109375 to 0.109375
- adapter_up_weight: bfloat16 [2048, 64], P('mp'), may hold values from -0.75 to 0.75
- actions: int32 [512, 32, 8], P(('dp', 'mp')), may hold values from 0 to 2047
- agent_present_mask: int32 [512, 32, 8], P(('dp', 'mp')), may hold values 0 or 1
- behaviour_log_prob: float32 [512, 32, 8], P(('dp', 'mp')), may hold values from -16 to -9
- advantages: float32 [512, 32, 8], P(('dp', 'mp')), may hold values from -4 to 4
Outputs:
- grad_down: float32 [3072, 64], P('mp')
- grad_up: float32 [2048, 64], P('mp')
All inputs are finite; a program needn't handle non-finite values. No bound on the sum of `agent_present_mask` on one device may be relied on, other than what follows from the above.
Results may differ from a plain program's by a relative error of at most 0.008.
Values may be sent and summed in bfloat16 or wider, within the bound.
No kernel may reach another device: no remote copies, remote signals or barrier semaphores. Data moves between devices by JAX's collectives and lax.ppermute only.
A program may use at most 64 MiB of HBM per device.

v0:
```python
import jax
import jax.numpy as jnp
from jax import lax
from jax.sharding import PartitionSpec as P

NORM_EPS = 1e-05
CLIP_LOG = 2.0
KL_COEF = 0.25


def normalize(hidden, gain):
    values = hidden.astype(jnp.float32)
    mean_square = jnp.mean(values * values, axis=-1, keepdims=True)
    return (values * lax.rsqrt(mean_square + NORM_EPS) * gain).astype(jnp.bfloat16)


def log_probs(policy_logits):
    return policy_logits - jnp.log(jnp.sum(jnp.exp(policy_logits), axis=-1, keepdims=True))


def rows_loss(policy_logits, ref_logp, chosen_ids, mask_rows, old_rows, adv_rows):
    logp = log_probs(policy_logits)
    picked = lax.broadcasted_iota(jnp.int32, policy_logits.shape, 1) == chosen_ids[:, None]
    chosen = jnp.sum(jnp.where(picked, logp, 0.0), axis=-1)
    surrogate = adv_rows * jnp.exp(CLIP_LOG * jnp.tanh((chosen - old_rows) / CLIP_LOG))
    divergence = jnp.sum(jnp.exp(logp) * (logp - ref_logp.astype(policy_logits.dtype)), axis=-1)
    return jnp.sum(mask_rows.astype(policy_logits.dtype) * (KL_COEF * divergence - surrogate))


def local(
    reference_hidden_states,
    policy_hidden_states,
    reference_norm_gain,
    policy_norm_gain,
    action_head_weight,
    adapter_down_weight,
    adapter_up_weight,
    actions,
    agent_present_mask,
    behaviour_log_prob,
    advantages,
):
    width = reference_hidden_states.shape[-1]
    up_factor_whole = lax.all_gather(adapter_up_weight, "mp", axis=0, tiled=True)
    ref_rows = lax.all_to_all(
        reference_hidden_states, "mp", split_axis=0, concat_axis=1, tiled=True
    )
    ref_normed = normalize(ref_rows, reference_norm_gain).reshape(-1, width)
    policy_normed_hidden = normalize(policy_hidden_states, policy_norm_gain).reshape(-1, width)
    weight_rows = lax.all_gather(action_head_weight, "mp", axis=0, tiled=True)
    down_factor_rows = lax.all_gather(adapter_down_weight, "mp", axis=0, tiled=True)
    ref_logits = jnp.dot(ref_normed, weight_rows, preferred_element_type=jnp.float32)
    base_logits = jnp.dot(policy_normed_hidden, weight_rows, preferred_element_type=jnp.float32)
    low_sum = jnp.dot(policy_normed_hidden, down_factor_rows, preferred_element_type=jnp.float32)
    ref_logp = log_probs(ref_logits).astype(jnp.bfloat16)
    adapter_product = low_sum.astype(jnp.bfloat16)
    policy_logits = base_logits + lax.dot_general(
        adapter_product,
        up_factor_whole,
        (((1,), (1,)), ((), ())),
        preferred_element_type=jnp.float32,
    )
    logit_slopes = jax.grad(rows_loss)(
        policy_logits,
        ref_logp,
        actions.reshape(-1),
        agent_present_mask.reshape(-1),
        behaviour_log_prob.reshape(-1),
        advantages.reshape(-1),
    ).astype(jnp.bfloat16)
    up_grad = lax.dot_general(
        logit_slopes, adapter_product, (((0,), (0,)), ((), ())), preferred_element_type=jnp.float32
    )
    adapter_slopes = jnp.dot(
        logit_slopes, up_factor_whole, preferred_element_type=jnp.float32
    ).astype(jnp.bfloat16)
    down_grad = lax.dot_general(
        policy_normed_hidden,
        adapter_slopes,
        (((0,), (0,)), ((), ())),
        preferred_element_type=jnp.float32,
    )
    whole_grads = lax.psum((down_grad, up_grad), "dp")
    down_out, up_out = (
        lax.psum_scatter(whole_grads[0], "mp", scatter_dimension=0, tiled=True),
        lax.psum_scatter(whole_grads[1], "mp", scatter_dimension=0, tiled=True),
    )
    return (down_out, up_out)


def solution(mesh):
    placed = (
        P("dp", "mp", None, None),
        P(("dp", "mp"), None, None, None),
        P(),
        P(),
        P("mp", None),
        P("mp", None),
        P("mp", None),
        P(("dp", "mp"), None, None),
        P(("dp", "mp"), None, None),
        P(("dp", "mp"), None, None),
        P(("dp", "mp"), None, None),
    )
    return jax.shard_map(
        local, mesh=mesh, in_specs=placed, out_specs=(P("mp", None), P("mp", None)), check_vma=False
    )
```

profile of v0, /device:TPU:1, one launch (start us, length us, event | category | flops | bytes accessed | tf_op | source)
XLA Modules:
  0.0 917.0 jit_solution(1551743865094891437)
XLA Ops:
  7.3 0.7 all-gather.3.cloned.1.call-update
  7.9 18.4 %all-to-all-start = ((bf16[16,2,8,3072]{3,2,1,0:T(8,128)(2,1)}), bf16[16,2,8,3072]{3,2,1,0:T(8,128)(2,1)S(1)}, u32[]{:S(2)}, u32[]{:S(2)}) async-start(bf16[16,2,8,3072]{3,2,1,0:T(8,128)(2,1)} %param.11), calls=%async_computation | async-start | bytes 3145728 | tf_op jit(solution)/shard_map/all_to_all | solution.py:45
  26.5 0.1 copy.18
  26.5 0.1 mul.97
  26.7 0.1 mul.107
  26.9 0.1 eq.10
  27.1 0.1 reshape.93
  27.2 166.1 %all-gather = bf16[16,192,64]{1,2,0:T(8,128)(2,1)S(1)} all-gather(bf16[1,192,64]{1,2,0:T(8,128)(2,1)S(1)} %bitcast.25), channel_id=1, replica_groups=mesh['dp'=32,'mp'=16] {'mp'}, dimensions={0}, use_global_device_ids=true | all-gather | bytes 417792 | tf_op jit(solution)/shard_map/all_gather | solution.py:51
  193.3 1.1 copy.19
  194.4 2.5 reshape.96
  196.8 84.3 %all_gather.11 = bf16[2048,64]{0,1:T(8,128)(2,1)S(1)} all-gather(bf16[128,64]{0,1:T(8,128)(2,1)S(1)} %copy-done.2), channel_id=1, replica_groups=mesh['dp'=32,'mp'=16] {'mp'}, dimensions={0}, use_global_device_ids=true | all-gather | bytes 278528 | tf_op jit(solution)/shard_map/all_gather | solution.py:44
  281.2 0.4 fusion
  281.6 1.7 convolution_convert_fusion.1
  283.3 0.4 multiply_reduce_fusion
  283.7 0.1 rsqrt.21
  283.8 1.7 fusion.4
  285.5 84.7 %all-gather.3.cloned.1.call-done = bf16[3072,2048]{1,0:T(8,128)(2,1)} async-done(((bf16[192,2048]{1,0:T(8,128)(2,1)}), bf16[3072,2048]{1,0:T(8,128)(2,1)}) %all-gather.3.cloned.1.call-update) | async-done | bytes 12582928 | tf_op jit(solution)/shard_map/all_gather | solution.py:50
  370.2 7.2 exponential_reduce_fusion
  377.3 1.4 copy-done.9
  378.8 3.6 fusion.9
  382.4 0.6 exponential_reduce_fusion.1
  382.9 0.4 select_reduce_fusion
  383.4 1.0 fusion.11
  384.5 0.4 add_convert_fusion
  384.8 2.7 fusion.6
  387.6 1.1 fusion.12
  388.7 152.0 %reduce-scatter.7.cloned.1.call-done = f32[192,64]{1,0:T(8,128)} async-done(((f32[3072,64]{1,0:T(8,128)}), f32[192,64]{1,0:T(8,128)}) %reduce-scatter.7.cloned.1.call-update) | async-done | bytes 49168
  540.8 1.6 copy.24
  542.4 108.2 %reduce-scatter.5.cloned.1.call-done = f32[128,64]{0,1:T(8,128)} async-done(((f32[2048,64]{0,1:T(8,128)}), f32[128,64]{0,1:T(8,128)}) %reduce-scatter.5.cloned.1.call-update) | async-done | bytes 32784 | tf_op jit(solution)/shard_map/reduce_scatter | solution.py:86
  650.6 257.0 %all-reduce.3.cloned.1.call-done = (f32[192,64]{0,1:T(8,128)}, f32[128,64]{0,1:T(8,128)}) async-done(((f32[192,64]{0,1:T(8,128)}, f32[128,64]{0,1:T(8,128)}), (f32[192,64]{0,1:T(8,128)}, f32[128,64]{0,1:T(8,128)})) %all-reduce.3.cloned.1.call-update) | async-done | bytes 81936 | tf_op jit(solution)/shard_map/psum | solution.py:83
  907.6 1.5 copy.27
  909.1 1.4 copy.28
  (37 shorter events, 0.6 us)
Async XLA Ops:
  7.2 19.3 %copy-start.8 = (f32[1,32,8]{1,2,0:T(8,128)S(1)}, f32[1,32,8]{1,2,0:T(8,128)}, u32[]{:S(2)}) copy-start(f32[1,32,8]{1,2,0:T(8,128)} %param.21) | copy-start | bytes 3076
  7.2 19.3 %copy-start.7 = (s32[1,32,8]{1,2,0:T(8,128)S(1)}, s32[1,32,8]{1,2,0:T(8,128)}, u32[]{:S(2)}) copy-start(s32[1,32,8]{1,2,0:T(8,128)} %param.19) | copy-start | bytes 3076
  7.2 19.6 %copy-start.5 = (s32[1,32,8]{1,2,0:T(8,128)S(1)}, s32[1,32,8]{1,2,0:T(8,128)}, u32[]{:S(2)}) copy-start(s32[1,32,8]{1,2,0:T(8,128)} %param.18) | copy-start | bytes 3076
  7.2 19.8 %copy-start.6 = (f32[1,32,8]{1,2,0:T(8,128)S(1)}, f32[1,32,8]{1,2,0:T(8,128)}, u32[]{:S(2)}) copy-start(f32[1,32,8]{1,2,0:T(8,128)} %param.20) | copy-start | bytes 3076
  7.2 19.9 %copy-start.1 = (bf16[192,64]{0,1:T(8,128)(2,1)S(1)}, bf16[192,64]{0,1:T(8,128)(2,1)}, u32[]{:S(2)}) copy-start(bf16[192,64]{0,1:T(8,128)(2,1)} %param.16) | copy-start | bytes 73732
  7.2 362.9 %all-gather.3.cloned.1.call-start = ((), (), s32[]{:S(2)}) async-start(), calls=%async_computation.3 | async-start | bytes 13369344 | tf_op jit(solution)/shard_map/all_gather | solution.py:50
  7.9 275.3 %all-to-all-start = ((bf16[16,2,8,3072]{3,2,1,0:T(8,128)(2,1)}), bf16[16,2,8,3072]{3,2,1,0:T(8,128)(2,1)S(1)}, u32[]{:S(2)}, u32[]{:S(2)}) async-start(bf16[16,2,8,3072]{3,2,1,0:T(8,128)(2,1)} %param.11), calls=%async_computation | async-start | bytes 3145728 | tf_op jit(solution)/shard_map/all_to_all | solution.py:45
  26.3 170.5 %copy-start.2 = (bf16[128,64]{0,1:T(8,128)(2,1)S(1)}, bf16[128,64]{0,1:T(8,128)(2,1)}, u32[]{:S(2)}) copy-start(bf16[128,64]{0,1:T(8,128)(2,1)} %param.17) | copy-start | bytes 49156
  26.4 254.8 %copy-start = (bf16[1,32,8,3072]{3,2,1,0:T(8,128)(2,1)S(1)}, bf16[1,32,8,3072]{3,2,1,0:T(8,128)(2,1)}, u32[]{:S(2)}) copy-start(bf16[1,32,8,3072]{3,2,1,0:T(8,128)(2,1)} %param.12) | copy-start | bytes 4718596
  26.4 514.4 %reduce-scatter.7.cloned.1.call-start = ((), (), s32[]{:S(2)}) async-start(), calls=%async_computation.5 | async-start | bytes 1671168
  27.1 254.4 %copy-start.4 = (f32[3072]{0:T(1024)S(1)}, f32[3072]{0:T(1024)}, u32[]{:S(2)}) copy-start(f32[3072]{0:T(1024)} %param.14) | copy-start | bytes 36868
  281.6 2.2 copy-start.3
  370.2 8.6 copy-start.9
  387.5 263.0 %reduce-scatter.5.cloned.1.call-start = ((), (), s32[]{:S(2)}) async-start(), calls=%async_computation.4 | async-start | bytes 557056 | tf_op jit(solution)/shard_map/reduce_scatter | solution.py:86
  388.7 518.9 %all-reduce.3.cloned.1.call-start = ((), (), s32[]{:S(2)}) async-start(), calls=%async_computation.6 | async-start | bytes 196608 | tf_op jit(solution)/shard_map/psum | solution.py:83
Sparse Core Ops, SparseCore 0:
  11.1 359.0 all-gather.2
  387.6 153.0 reduce-scatter.6
  544.8 105.6 reduce-scatter.4
  654.2 253.3 all-reduce.2
where the time goes:
time: 918 us; the launch traced here: 917 us
  waiting for transfers between devices  603 us (66%)
  blocking collectives  250 us (27%)
  starting transfers between devices  18.6 us (2%)
  matrix products  16.7 us (2%)
  between operations  14 us (2%)
  local copies, waits for them, and re-layouts  10.3 us (1%)
    psum x1, waiting for transfers between devices, local(): whole_grads = lax.psum((down_grad, up_grad), 'dp')  257 us
    all_gather x1, blocking collectives, local(): lax.all_gather(adapter_down_weight, 'mp', axis=0, tiled=True)  166 us
    unnamed x5, waiting for transfers between devices  153 us
    reduce_scatter x1, waiting for transfers between devices, local(): lax.psum_scatter(whole_grads[1], 'mp', scatter_dimension=0, tiled=True)  108 us
    all_gather x1, waiting for transfers between devices, local(): weight_rows = lax.all_gather(action_head_weight, 'mp', axis=0, tiled=True)  84.7 us
    all_gather x1, blocking collectives, local(): lax.all_gather(adapter_up_weight, 'mp', axis=0, tiled=True)  84.3 us
    all_to_all x1, starting transfers between devices, local(): lax.all_to_all(reference_hidden_states, 'mp', split_axis=0, concat_axis=1...  18.4 us
  transfers between devices with their start and end apart: 5, of which 4 were waited for; matrix products, arithmetic and copies ran while one was open for 1% of the time, Pallas kernels for 0%

commit v1 on v0

v1 whole, which is shorter than its diff:
```python
import functools

import jax
import jax.numpy as jnp
import numpy as np
from jax import lax
from jax.experimental import pallas as pl
from jax.experimental.pallas import tpu as pltpu
from jax.sharding import Mesh, PartitionSpec as P

NORM_EPS = 1e-05
CLIP_LOG = 2.0
KL_COEF = 0.25

X, ZL, C, Y, ZH = 4, 4, 2, 4, 4
WIDTH = 3072
TOKENS = 2048
RANK = 64
ROWS = 256
KY = WIDTH // Y
KM = KY // ZH
TM = TOKENS // (Y * ZH)
NB = TOKENS // (C * X)
PIECE = KY + ZH * 16
SHIFTS = (0, 1, 3, 2)
LANES = 384

bf16 = jnp.bfloat16
f32 = jnp.float32


def pairs(step):
    sizes = (X, C, Y)
    found = []
    for index in np.ndindex(*sizes):
        to = tuple(t % s for t, s in zip(step(*index), sizes))
        found.append(
            (int(np.ravel_multi_index(index, sizes)), int(np.ravel_multi_index(to, sizes)))
        )
    return found


def shift_first(v, k):
    return lax.ppermute(v, ("x", "c", "y"), pairs(lambda x, c, y: (x + k * (c == 0), c, y + k * (c == 1))))


def shift_second(v, k):
    return lax.ppermute(v, ("x", "c", "y"), pairs(lambda x, c, y: (x + k * (c == 1), c, y + k * (c == 0))))


def swap_cores(v):
    return lax.ppermute(v, "c", [(0, 1), (1, 0)])


def bdot(a, b, dims):
    return lax.dot_general(a, b, (dims, ((), ())), preferred_element_type=f32)


def kernel(
    place, pol_hbm, ref_hbm, pol_gain, ref_gain, rows8,
    p0, p1, p2, p3, p4, p5, p6, p7,
    keep, give,
    held, normed, acc, up, down, slopes, low_t, grad, hid, sems,
):
    x, y, c = place[0], place[1], place[2]
    parts = (p0, p1, p2, p3, p4, p5, p6, p7)
    first = [
        pltpu.make_async_copy(pol_hbm, hid.at[0], sems.at[8]),
        pltpu.make_async_copy(ref_hbm, hid.at[1], sems.at[9]),
    ]
    copies = [pltpu.make_async_copy(parts[i], held.at[i], sems.at[i]) for i in range(8)]
    for copy in first + copies:
        copy.start()

    acc[...] = jnp.zeros_like(acc)
    step = 32
    for which, gain in ((0, pol_gain), (1, ref_gain)):
        first[which].wait()

        def norm(i, carry, which=which, gain=gain):
            at = pl.ds(pl.multiple_of(i * step, step), step)
            v = hid[which, at, :].astype(f32)
            ms = jnp.sum(v * v, axis=-1, keepdims=True) * (1.0 / WIDTH)
            n = (v * lax.rsqrt(ms + NORM_EPS) * gain[...]).astype(bf16)
            for k in range(Y):
                normed[which, k, at, :] = n[:, k * KY : (k + 1) * KY]
            return carry

        lax.fori_loop(0, ROWS // step, norm, 0)

    for i in range(8):
        copies[i].wait()
        core = c if i < 4 else 1 - c
        k2 = SHIFTS[i % 4]

        def block(q, carry, i=i, core=core, k2=k2):
            k1 = jnp.where(q == 2, 3, jnp.where(q == 3, 2, q))
            kx = jnp.where(core == 0, k1, k2)
            ky = jnp.where(core == 0, k2, k1)
            xq = lax.rem(x + X - kx, X)
            ys = lax.rem(y + Y - ky, Y)
            j = core * X + xq
            w = held[i, q, 0:KY, :]
            for which in range(2):
                acc[which, j] += bdot(normed[which, ys], w, ((1,), (0,)))
            at = pl.ds(pl.multiple_of(xq * 16, 16), 16)
            e = held[i, q, KY:PIECE, :]

            @pl.when(core == 0)
            def _():
                for z in range(ZH):
                    up[ys, at, z * TM : (z + 1) * TM] = e[z * 16 : (z + 1) * 16, 0:TM]

            @pl.when(core == 1)
            def _():
                down[ys, at, :] = jnp.concatenate(
                    [e[z * 16 : (z + 1) * 16, 0:KM] for z in range(ZH)], axis=1
                )

            return carry

        lax.fori_loop(0, 4, block, 0)

    low = jnp.zeros((ROWS, RANK), f32)
    for k in range(Y):
        low += bdot(normed[0, k], down[k], ((1,), (1,)))
    low16 = low.astype(bf16)
    low_t[...] = low.T.astype(bf16)

    cols = rows8[...].T
    acts = cols[:, 0:1].astype(jnp.int32)
    mask, old, adv = cols[:, 1:2], cols[:, 2:3], cols[:, 3:4]
    iota = lax.broadcasted_iota(jnp.int32, (ROWS, NB), 1)

    def up_part(j):
        return up[j // 2, :, (j % 2) * NB : (j % 2 + 1) * NB]

    s_pol = jnp.zeros((ROWS, 1), f32)
    s_ref = jnp.zeros((ROWS, 1), f32)
    hit = jnp.zeros((ROWS, 1), f32)
    for j in range(8):
        v = acc[0, j] + bdot(low16, up_part(j), ((1,), (0,)))
        acc[0, j] = v
        s_pol += jnp.sum(jnp.exp(v), axis=-1, keepdims=True)
        hit += jnp.sum(jnp.where(iota == acts - j * NB, v, 0.0), axis=-1, keepdims=True)
        s_ref += jnp.sum(jnp.exp(acc[1, j]), axis=-1, keepdims=True)
    lse_pol, lse_ref = jnp.log(s_pol), jnp.log(s_ref)
    taken = hit - lse_pol
    t = jnp.tanh((taken - old) / CLIP_LOG)
    pull = mask * (adv * jnp.exp(CLIP_LOG * t) * (1.0 - t * t))
    div = jnp.zeros((ROWS, 1), f32)
    for j in range(8):
        logp = acc[0, j] - lse_pol
        gap = logp - (acc[1, j] - lse_ref).astype(bf16).astype(f32)
        p = jnp.exp(logp)
        div += jnp.sum(p * gap, axis=-1, keepdims=True)
        acc[0, j] = p
        acc[1, j] = gap
    scale = mask * KL_COEF
    base = pull - scale * div
    low_slopes = jnp.zeros((ROWS, RANK), f32)
    for j in range(8):
        s = acc[0, j] * (scale * acc[1, j] + base) - jnp.where(iota == acts - j * NB, pull, 0.0)
        s16 = s.astype(bf16)
        grad[:, j * NB : (j + 1) * NB] = bdot(low_t[...], s16, ((1,), (0,)))
        low_slopes += bdot(s16, up_part(j), ((1,), (1,)))
    low_slopes_t = low_slopes.T.astype(bf16)
    for k in range(Y):
        grad[:, TOKENS + k * KY : TOKENS + (k + 1) * KY] = bdot(low_slopes_t, normed[0, k], ((1,), (0,)))

    blank = jnp.zeros((8, LANES - TM - KM), f32)
    for out, core in ((keep, c), (give, 1 - c)):
        for xx in range(X):
            at = pl.ds(pl.multiple_of((xx * C + core) * 8, 8), 8)
            for m in range(Y * ZH):
                out[xx, m] = jnp.concatenate(
                    [
                        grad[at, m * TM : (m + 1) * TM],
                        grad[at, TOKENS + m * KM : TOKENS + (m + 1) * KM],
                        blank,
                    ],
                    axis=1,
                )


def local(ref_hidden, pol_hidden, ref_gain, pol_gain, head, down_w, up_w, actions, present, old, adv):
    x, y, c = lax.axis_index("x"), lax.axis_index("y"), lax.axis_index("c")
    piece = lax.dynamic_slice(head, (0, (c * X + x) * NB), (KM, NB))
    up_t = jnp.pad(up_w.T, ((0, 0), (0, NB - TM)))
    down_t = jnp.pad(down_w.T, ((0, 0), (0, NB - KM)))
    extra = lax.dynamic_slice(jnp.where(c == 0, up_t, down_t), (x * 16, 0), (16, NB))
    piece = jnp.concatenate([piece, extra], axis=0)
    along_z = lax.all_to_all(
        jnp.broadcast_to(piece[None], (ZH, KM + 16, NB)), "zh", 0, 0, tiled=True
    )
    mine = jnp.concatenate(
        [along_z[:, :KM].reshape(KY, NB), along_z[:, KM:].reshape(ZH * 16, NB)], axis=0
    )
    four = jnp.stack([mine] + [shift_first(mine, k) for k in SHIFTS[1:]])
    own = [four] + [shift_second(four, k) for k in SHIFTS[1:]]
    other = [swap_cores(v) for v in own]

    ref_rows = lax.all_to_all(
        ref_hidden.reshape(Y * ZH, ROWS // (Y * ZH), WIDTH), ("y", "zh"), 0, 0, tiled=True
    ).reshape(ROWS, WIDTH)
    pol_rows = pol_hidden.reshape(ROWS, WIDTH)
    rows8 = jnp.stack(
        [v.reshape(ROWS).astype(f32) for v in (actions, present, old, adv)]
        + [jnp.zeros((ROWS,), f32)] * 4
    )
    place = jnp.stack([x, y, c]).astype(jnp.int32)

    vmem = pl.BlockSpec(memory_space=pltpu.VMEM)
    hbm = pl.BlockSpec(memory_space=pl.ANY)
    out = jax.ShapeDtypeStruct((X, Y * ZH, 8, LANES), f32)
    keep, give = pl.pallas_call(
        kernel,
        out_shape=(out, out),
        in_specs=[pl.BlockSpec(memory_space=pltpu.SMEM), hbm, hbm, vmem, vmem, vmem] + [hbm] * 8,
        out_specs=(vmem, vmem),
        scratch_shapes=[
            pltpu.VMEM((8, 4, PIECE, NB), bf16),
            pltpu.VMEM((2, Y, ROWS, KY), bf16),
            pltpu.VMEM((2, C * X, ROWS, NB), f32),
            pltpu.VMEM((Y, RANK, TOKENS // Y), bf16),
            pltpu.VMEM((Y, RANK, KY), bf16),
            pltpu.VMEM((8, 128), bf16),
            pltpu.VMEM((RANK, ROWS), bf16),
            pltpu.VMEM((RANK, TOKENS + WIDTH), f32),
            pltpu.VMEM((2, ROWS, WIDTH), bf16),
            pltpu.SemaphoreType.DMA((10,)),
        ],
        compiler_params=pltpu.CompilerParams(vmem_limit_bytes=36 * 1024 * 1024),
        cost_estimate=pl.CostEstimate(
            flops=4 * ROWS * WIDTH * TOKENS, bytes_accessed=18 << 20, transcendentals=3 * ROWS * TOKENS
        ),
    )(
        place, pol_rows, ref_rows,
        pol_gain.reshape(1, WIDTH), ref_gain.reshape(1, WIDTH), rows8, *own, *other,
    )

    part = keep + swap_cores(give)
    part = lax.all_to_all(part.reshape(X * Y, ZH, 8, LANES), ("x", "y"), 0, 0, tiled=True).sum(0)
    part = jnp.broadcast_to(part[None], (ZL, ZH, 8, LANES)).reshape(ZL * ZH, 8, LANES)
    part = lax.all_to_all(part, ("zl", "zh"), 0, 0, tiled=True).sum(0)
    whole = lax.all_to_all(
        jnp.broadcast_to(part[None], (X * C, 8, LANES)), ("x", "c"), 0, 0, tiled=True
    ).reshape(RANK, LANES)
    return whole[:, TM : TM + KM].T, whole[:, :TM].T


def solution(mesh):
    wide = Mesh(mesh.devices.reshape(X, ZL, C, Y, ZH), ("x", "zl", "c", "y", "zh"))
    dp, mp = ("x", "zl", "c"), ("y", "zh")
    placed = (
        P(dp, mp, None, None),
        P(dp + mp, None, None, None),
        P(),
        P(),
        P(mp, None),
        P(mp, None),
        P(mp, None),
        P(dp + mp, None, None),
        P(dp + mp, None, None),
        P(dp + mp, None, None),
        P(dp + mp, None, None),
    )
    return jax.shard_map(
        local, mesh=wide, in_specs=placed, out_specs=(P(mp, None), P(mp, None)), check_vma=False
    )
```

time: 918 us -> 228 us (0.25)
  waiting for transfers between devices: 603 us -> 51 us
  blocking collectives: 250 us -> 107 us
  starting transfers between devices: 18.6 us -> 40.6 us
  Pallas kernels: 0 us -> 21.4 us
  matrix products: 16.7 us -> 0 us
  between operations: 14 us -> 0.94 us
    psum x1 -> x0, waiting for transfers between devices: 257 us -> none  [local(): whole_grads = lax.psum((down_grad, up_grad), 'dp')]
    all_gather x2 -> x0, blocking collectives: 250 us -> none  [the longest x1 166 us: local(): lax.all_gather(adapter_down_weight, 'mp', axis=0, tiled=True)]
    unnamed x5 -> x0, waiting for transfers between devices: 153 us -> none
    reduce_scatter x1 -> x0, waiting for transfers between devices: 108 us -> none  [local(): lax.psum_scatter(whole_grads[1], 'mp', scatter_dimension=0, tiled=True)]
    all_to_all x0 -> x4, blocking collectives: none -> 107 us  [the longest x1 40 us: local(): part = lax.all_to_all(part, ('zl', 'zh'), 0, 0, tiled=True).sum(0)]
    all_gather x1 -> x0, waiting for transfers between devices: 84.7 us -> none  [local(): weight_rows = lax.all_gather(action_head_weight, 'mp', axis=0, tiled=True)]
    ppermute x0 -> x11, waiting for transfers between devices: none -> 51 us  [the longest x3 28 us: shift_second(): lax.ppermute(v, ('x', 'c', 'y'), pairs(lambda x, c, y: (x + k * (c == 1),...]
    ppermute x0 -> x11, starting transfers between devices: none -> 31.2 us  [the longest x5 11.2 us: swap_cores(): return lax.ppermute(v, 'c', [(0, 1), (1, 0)])]
  transfers between devices with their start and end apart: 5 -> 12, of which waited for: 4 -> 8; matrix products, arithmetic and copies ran while one was open for 1% -> 0% of each run, Pallas kernels for 0% -> 0%
where the time goes in v1:
time: 228 us; the launch traced here: 227 us
  blocking collectives  107 us (47%)
  waiting for transfers between devices  51 us (22%)
  starting transfers between devices  40.6 us (18%)
  Pallas kernels  21.4 us (9%)
  local copies, waits for them, and re-layouts  4.59 us (2%)
    all_to_all x1, blocking collectives, local(): part = lax.all_to_all(part, ('zl', 'zh'), 0, 0, tiled=True).sum(0)  40 us
    all_to_all x1, blocking collectives, local(): lax.all_to_all(jnp.broadcast_to(piece[None], (ZH, KM + 16, NB)), 'zh', 0,...  37.1 us
    ppermute x3, waiting for transfers between devices, shift_second(): lax.ppermute(v, ('x', 'c', 'y'), pairs(lambda x, c, y: (x + k * (c == 1),...  28 us
    pallas_call x1, Pallas kernels, local(): pl.pallas_call(kernel, out_shape=(out, out), in_specs=[pl.BlockSpec(memor...  21.4 us
    all_to_all x1, blocking collectives, local(): lax.all_to_all(part.reshape(X * Y, ZH, 8, LANES), ('x', 'y'), 0, 0, tiled...  17.9 us
    ppermute x3, waiting for transfers between devices, shift_first(): lax.ppermute(v, ('x', 'c', 'y'), pairs(lambda x, c, y: (x + k * (c == 0),...  17.8 us
    all_to_all x1, blocking collectives, local(): lax.all_to_all(jnp.broadcast_to(part[None], (X * C, 8, LANES)), ('x', 'c'...  12.1 us
    ppermute x5, starting transfers between devices, swap_cores(): return lax.ppermute(v, 'c', [(0, 1), (1, 0)])  11.2 us
  transfers between devices with their start and end apart: 12, of which 8 were waited for; matrix products, arithmetic and copies ran while one was open for 0% of the time, Pallas kernels for 0%

profile of v1, /device:TPU:1, one launch (start us, length us, event | category | flops | bytes accessed | tf_op | source)
XLA Modules:
  0.0 226.9 jit_solution(14399980359876054436)
XLA Ops:
  0.7 1.1 copy-done
  1.8 0.7 fusion
  2.6 37.1 %all_to_all.25 = bf16[4,208,256]{2,1,0:T(8,128)(2,1)S(1)} all-to-all(bf16[4,208,256]{2,1,0:T(8,128)(2,1)S(1)} %broadcast_in_dim.6), channel_id=1, replica_groups=mesh['x'=4,'zl'=4,'c'=2,'y'=4,'zh'=4] {'zh'}, dimensions={0} | all-to-all | bytes 851968 | tf_op jit(solution)/shard_map/all_to_all | solution.py:193
  39.7 9.4 %all-to-all-start = ((bf16[16,16,3072]{2,1,0:T(8,128)(2,1)}), bf16[16,16,3072]{2,1,0:T(8,128)(2,1)}, u32[]{:S(2)}, u32[]{:S(2)}) async-start(bf16[16,16,3072]{2,1,0:T(8,128)(2,1)} %bitcast.4), calls=%async_computation | async-start | bytes 3145728 | tf_op jit(solution)/shard_map/all_to_all | solution.py:203
  49.2 4.4 %collective-permute-start.1 = (bf16[832,256]{1,0:T(8,128)(2,1)S(1)}, bf16[832,256]{1,0:T(8,128)(2,1)S(1)}, u32[]{:S(2)}, u32[]{:S(2)}) collective-permute-start(bf16[832,256]{1,0:T(8,128)(2,1)S(1)} %get-tuple-element.7), channel_id=1, source_target_pairs={{0,384},{4,388},{8,392},{12,396},{16,28},{20,16},{24,20},{28,24},{... | collective-permute-start | bytes 1277960 | tf_op jit(solution)/shard_map/ppermute | solution.py:44
  53.7 1.9 collective-permute-start
  55.6 3.7 %collective-permute-start.2 = (bf16[832,256]{1,0:T(8,128)(2,1)S(1)}, bf16[832,256]{1,0:T(8,128)(2,1)S(1)}, u32[]{:S(2)}, u32[]{:S(2)}) collective-permute-start(bf16[832,256]{1,0:T(8,128)(2,1)S(1)} %get-tuple-element.7), channel_id=1, source_target_pairs={{0,256},{4,260},{8,264},{12,268},{16,24},{20,28},{24,16},{28,20},{... | collective-permute-start | bytes 1277960 | tf_op jit(solution)/shard_map/ppermute | solution.py:44
  59.3 2.0 collective-permute-done.1
  61.2 8.1 %collective-permute-done = bf16[832,256]{1,0:T(8,128)(2,1)S(1)} collective-permute-done((bf16[832,256]{1,0:T(8,128)(2,1)S(1)}, bf16[832,256]{1,0:T(8,128)(2,1)S(1)}, u32[]{:S(2)}, u32[]{:S(2)}) %collective-permute-start) | collective-permute-done | bytes 426016 | tf_op jit(solution)/shard_map/ppermute | solution.py:44
  69.3 7.8 %collective-permute-done.2 = bf16[832,256]{1,0:T(8,128)(2,1)S(1)} collective-permute-done((bf16[832,256]{1,0:T(8,128)(2,1)S(1)}, bf16[832,256]{1,0:T(8,128)(2,1)S(1)}, u32[]{:S(2)}, u32[]{:S(2)}) %collective-permute-start.2) | collective-permute-done | bytes 426016 | tf_op jit(solution)/shard_map/ppermute | solution.py:44
  77.1 0.2 pad_maximum_fusion.p0
  77.4 4.7 %collective-permute-start.5 = (bf16[4,832,256]{2,1,0:T(8,128)(2,1)S(1)}, bf16[4,832,256]{2,1,0:T(8,128)(2,1)}, u32[]{:S(2)}, u32[]{:S(2)}) collective-permute-start(bf16[4,832,256]{2,1,0:T(8,128)(2,1)S(1)} %pad_maximum_fusion.p0), channel_id=1, source_target_pairs={{0,8},{4,12},{8,0},{12,4},{16,272},{20,276},{24,280},{28,284},{128... | collective-permute-start | bytes 5111816 | tf_op jit(solution)/shard_map/ppermute | solution.py:48
  82.0 2.8 %collective-permute-start.4 = (bf16[4,832,256]{2,1,0:T(8,128)(2,1)S(1)}, bf16[4,832,256]{2,1,0:T(8,128)(2,1)}, u32[]{:S(2)}, u32[]{:S(2)}) collective-permute-start(bf16[4,832,256]{2,1,0:T(8,128)(2,1)S(1)} %pad_maximum_fusion.p0), channel_id=1, source_target_pairs={{0,12},{4,0},{8,4},{12,8},{16,400},{20,404},{24,408},{28,412},{128... | collective-permute-start | bytes 5111816 | tf_op jit(solution)/shard_map/ppermute | solution.py:48
  84.8 2.5 %collective-permute-start.3 = (bf16[4,832,256]{2,1,0:T(8,128)(2,1)S(1)}, bf16[4,832,256]{2,1,0:T(8,128)(2,1)}, u32[]{:S(2)}, u32[]{:S(2)}) collective-permute-start(bf16[4,832,256]{2,1,0:T(8,128)(2,1)S(1)} %pad_maximum_fusion.p0), channel_id=1, source_target_pairs={{0,4},{4,8},{8,12},{12,0},{16,144},{20,148},{24,152},{28,156},{128... | collective-permute-start | bytes 5111816 | tf_op jit(solution)/shard_map/ppermute | solution.py:48
  87.3 1.9 collective-permute-start.6
  89.2 12.6 %collective-permute-done.5.p3 = bf16[4,832,256]{2,1,0:T(8,128)(2,1)} collective-permute-done((bf16[4,832,256]{2,1,0:T(8,128)(2,1)S(1)}, bf16[4,832,256]{2,1,0:T(8,128)(2,1)}, u32[]{:S(2)}, u32[]{:S(2)}) %collective-permute-start.5) | collective-permute-done | bytes 1703968 | tf_op jit(solution)/shard_map/ppermute | solution.py:48
  101.9 2.9 %collective-permute-start.9 = (bf16[4,832,256]{2,1,0:T(8,128)(2,1)}, bf16[4,832,256]{2,1,0:T(8,128)(2,1)}, u32[]{:S(2)}, u32[]{:S(2)}) collective-permute-start(bf16[4,832,256]{2,1,0:T(8,128)(2,1)} %collective-permute-done.5.p3), channel_id=1, source_target_pairs={{0,16},{16,0},{1,17},{17,1},{2,18},{18,2},{3,19},{19,3},{4,20},{20... | collective-permute-start | bytes 5111816 | tf_op jit(solution)/shard_map/ppermute | solution.py:52
  104.8 15.4 %collective-permute-done.4.p2 = bf16[4,832,256]{2,1,0:T(8,128)(2,1)} collective-permute-done((bf16[4,832,256]{2,1,0:T(8,128)(2,1)S(1)}, bf16[4,832,256]{2,1,0:T(8,128)(2,1)}, u32[]{:S(2)}, u32[]{:S(2)}) %collective-permute-start.4) | collective-permute-done | bytes 1703968 | tf_op jit(solution)/shard_map/ppermute | solution.py:48
  120.2 1.9 collective-permute-start.8
  122.1 2.4 %collective-permute-start.7 = (bf16[4,832,256]{2,1,0:T(8,128)(2,1)}, bf16[4,832,256]{2,1,0:T(8,128)(2,1)}, u32[]{:S(2)}, u32[]{:S(2)}) collective-permute-start(bf16[4,832,256]{2,1,0:T(8,128)(2,1)} %collective-permute-done.3.p1), channel_id=1, source_target_pairs={{0,16},{16,0},{1,17},{17,1},{2,18},{18,2},{3,19},{19,3},{4,20},{20... | collective-permute-start | bytes 5111816 | tf_op jit(solution)/shard_map/ppermute | solution.py:52
  124.8 0.1 convert_element_type.31
  125.4 0.6 collective-permute-done.8.p6
  126.0 2.4 %collective-permute-done.7.p5 = bf16[4,832,256]{2,1,0:T(8,128)(2,1)} collective-permute-done((bf16[4,832,256]{2,1,0:T(8,128)(2,1)}, bf16[4,832,256]{2,1,0:T(8,128)(2,1)}, u32[]{:S(2)}, u32[]{:S(2)}) %collective-permute-start.7) | collective-permute-done | bytes 1703968 | tf_op jit(solution)/shard_map/ppermute | solution.py:52
  128.5 1.4 copy-done.1
  129.9 21.4 %shard_map.122 = (f32[4,16,8,384]{3,2,1,0:T(8,128)S(1)}, f32[4,16,8,384]{3,2,1,0:T(8,128)S(1)}) custom-call(s32[3]{0:T(128)S(1)} %pad_add_fusion.place, bf16[256,3072]{1,0:T(8,128)(2,1)S(1)} %bitcast.24, bf16[256,3072]{1,0:T(8,128)(2,1)} %bitcast.5.ref_hbm, f32[1,3072]{1,0:T(1,128)S(1)} %bitcast.25, f32[1,3072]{1,0:T(1,128)S(1)} %bitcast.26, ...), custom_call_target="tpu_custom_call" | custom-call | flops 6442450944 | bytes 18874368 | tf_op jit(solution)/shard_map/pallas_call | solution.py:216
  151.3 2.0 collective-permute-start.10
  153.4 2.1 collective-permute-done.10
  155.6 17.9 %all_to_all.26 = f32[16,4,8,384]{3,2,1,0:T(8,128)S(1)} all-to-all(f32[16,4,8,384]{3,2,1,0:T(8,128)S(1)} %bitcast.27), channel_id=1, replica_groups=mesh['x'=4,'zl'=4,'c'=2,'y'=4,'zh'=4] {'x','y'}, dimensions={0} | all-to-all | bytes 1572864 | tf_op jit(solution)/shard_map/all_to_all | solution.py:243
  173.5 40.0 %all_to_all.27 = f32[16,8,384]{2,1,0:T(8,128)S(1)} all-to-all(f32[16,8,384]{2,1,0:T(8,128)S(1)} %bitcast.29), channel_id=1, replica_groups=mesh['x'=4,'zl'=4,'c'=2,'y'=4,'zh'=4] {'zl','zh'}, dimensions={0} | all-to-all | bytes 393216 | tf_op jit(solution)/shard_map/all_to_all | solution.py:245
  213.6 12.1 %all_to_all.28 = f32[8,8,384]{2,1,0:T(8,128)S(1)} all-to-all(f32[8,8,384]{2,1,0:T(8,128)S(1)} %broadcast_in_dim.8), channel_id=1, replica_groups=mesh['x'=4,'zl'=4,'c'=2,'y'=4,'zh'=4] {'x','c'}, dimensions={0} | all-to-all | bytes 196608 | tf_op jit(solution)/shard_map/all_to_all | solution.py:246
  225.7 0.6 slice_bitcast_fusion.1
  226.3 0.6 slice_bitcast_fusion
  (41 shorter events, 1.0 us)
Async XLA Ops:
  0.6 1.1 copy-start
  39.7 88.8 %all-to-all-start = ((bf16[16,16,3072]{2,1,0:T(8,128)(2,1)}), bf16[16,16,3072]{2,1,0:T(8,128)(2,1)}, u32[]{:S(2)}, u32[]{:S(2)}) async-start(bf16[16,16,3072]{2,1,0:T(8,128)(2,1)} %bitcast.4), calls=%async_computation | async-start | bytes 3145728 | tf_op jit(solution)/shard_map/all_to_all | solution.py:203
  49.2 12.0 %collective-permute-start.1 = (bf16[832,256]{1,0:T(8,128)(2,1)S(1)}, bf16[832,256]{1,0:T(8,128)(2,1)S(1)}, u32[]{:S(2)}, u32[]{:S(2)}) collective-permute-start(bf16[832,256]{1,0:T(8,128)(2,1)S(1)} %get-tuple-element.7), channel_id=1, source_target_pairs={{0,384},{4,388},{8,392},{12,396},{16,28},{20,16},{24,20},{28,24},{... | collective-permute-start | bytes 1277960 | tf_op jit(solution)/shard_map/ppermute | solution.py:44
  53.7 15.6 %collective-permute-start = (bf16[832,256]{1,0:T(8,128)(2,1)S(1)}, bf16[832,256]{1,0:T(8,128)(2,1)S(1)}, u32[]{:S(2)}, u32[]{:S(2)}) collective-permute-start(bf16[832,256]{1,0:T(8,128)(2,1)S(1)} %get-tuple-element.7), channel_id=1, source_target_pairs={{0,128},{4,132},{8,136},{12,140},{16,20},{20,24},{24,28},{28,16},{... | collective-permute-start | bytes 1277960 | tf_op jit(solution)/shard_map/ppermute | solution.py:44
  55.6 21.5 %collective-permute-start.2 = (bf16[832,256]{1,0:T(8,128)(2,1)S(1)}, bf16[832,256]{1,0:T(8,128)(2,1)S(1)}, u32[]{:S(2)}, u32[]{:S(2)}) collective-permute-start(bf16[832,256]{1,0:T(8,128)(2,1)S(1)} %get-tuple-element.7), channel_id=1, source_target_pairs={{0,256},{4,260},{8,264},{12,268},{16,24},{20,28},{24,16},{28,20},{... | collective-permute-start | bytes 1277960 | tf_op jit(solution)/shard_map/ppermute | solution.py:44
  77.1 47.5 %copy-start.6 = (s32[1,32,8]{1,2,0:T(8,128)S(1)}, s32[1,32,8]{1,2,0:T(8,128)}, u32[]{:S(2)}) copy-start(s32[1,32,8]{1,2,0:T(8,128)} %param.18) | copy-start | bytes 3076
  77.1 47.5 %copy-start.7 = (s32[1,32,8]{1,2,0:T(8,128)S(1)}, s32[1,32,8]{1,2,0:T(8,128)}, u32[]{:S(2)}) copy-start(s32[1,32,8]{1,2,0:T(8,128)} %param.19) | copy-start | bytes 3076
  77.1 47.8 %copy-start.4 = (f32[1,32,8]{1,2,0:T(8,128)S(1)}, f32[1,32,8]{1,2,0:T(8,128)}, u32[]{:S(2)}) copy-start(f32[1,32,8]{1,2,0:T(8,128)} %param.20) | copy-start | bytes 3076
  77.1 48.0 %copy-start.5 = (f32[1,32,8]{1,2,0:T(8,128)S(1)}, f32[1,32,8]{1,2,0:T(8,128)}, u32[]{:S(2)}) copy-start(f32[1,32,8]{1,2,0:T(8,128)} %param.21) | copy-start | bytes 3076
  77.1 51.4 %copy-start.2 = (f32[3072]{0:T(1024)S(1)}, f32[3072]{0:T(1024)}, u32[]{:S(2)}) copy-start(f32[3072]{0:T(1024)} %param.14) | copy-start | bytes 36868
  77.1 51.4 %copy-start.3 = (f32[3072]{0:T(1024)S(1)}, f32[3072]{0:T(1024)}, u32[]{:S(2)}) copy-start(f32[3072]{0:T(1024)} %param.13) | copy-start | bytes 36868
  77.4 24.5 %collective-permute-start.5 = (bf16[4,832,256]{2,1,0:T(8,128)(2,1)S(1)}, bf16[4,832,256]{2,1,0:T(8,128)(2,1)}, u32[]{:S(2)}, u32[]{:S(2)}) collective-permute-start(bf16[4,832,256]{2,1,0:T(8,128)(2,1)S(1)} %pad_maximum_fusion.p0), channel_id=1, source_target_pairs={{0,8},{4,12},{8,0},{12,4},{16,272},{20,276},{24,280},{28,284},{128... | collective-permute-start | bytes 5111816 | tf_op jit(solution)/shard_map/ppermute | solution.py:48
  82.0 38.2 %collective-permute-start.4 = (bf16[4,832,256]{2,1,0:T(8,128)(2,1)S(1)}, bf16[4,832,256]{2,1,0:T(8,128)(2,1)}, u32[]{:S(2)}, u32[]{:S(2)}) collective-permute-start(bf16[4,832,256]{2,1,0:T(8,128)(2,1)S(1)} %pad_maximum_fusion.p0), channel_id=1, source_target_pairs={{0,12},{4,0},{8,4},{12,8},{16,400},{20,404},{24,408},{28,412},{128... | collective-permute-start | bytes 5111816 | tf_op jit(solution)/shard_map/ppermute | solution.py:48
  84.8 37.3 %collective-permute-start.3 = (bf16[4,832,256]{2,1,0:T(8,128)(2,1)S(1)}, bf16[4,832,256]{2,1,0:T(8,128)(2,1)}, u32[]{:S(2)}, u32[]{:S(2)}) collective-permute-start(bf16[4,832,256]{2,1,0:T(8,128)(2,1)S(1)} %pad_maximum_fusion.p0), channel_id=1, source_target_pairs={{0,4},{4,8},{8,12},{12,0},{16,144},{20,148},{24,152},{28,156},{128... | collective-permute-start | bytes 5111816 | tf_op jit(solution)/shard_map/ppermute | solution.py:48
  87.3 38.1 %collective-permute-start.6 = (bf16[4,832,256]{2,1,0:T(8,128)(2,1)S(1)}, bf16[4,832,256]{2,1,0:T(8,128)(2,1)}, u32[]{:S(2)}, u32[]{:S(2)}) collective-permute-start(bf16[4,832,256]{2,1,0:T(8,128)(2,1)S(1)} %pad_maximum_fusion.p0), channel_id=1, source_target_pairs={{0,16},{16,0},{1,17},{17,1},{2,18},{18,2},{3,19},{19,3},{4,20},{20... | collective-permute-start | bytes 5111816 | tf_op jit(solution)/shard_map/ppermute | solution.py:52
  101.9 23.5 %collective-permute-start.9 = (bf16[4,832,256]{2,1,0:T(8,128)(2,1)}, bf16[4,832,256]{2,1,0:T(8,128)(2,1)}, u32[]{:S(2)}, u32[]{:S(2)}) collective-permute-start(bf16[4,832,256]{2,1,0:T(8,128)(2,1)} %collective-permute-done.5.p3), channel_id=1, source_target_pairs={{0,16},{16,0},{1,17},{17,1},{2,18},{18,2},{3,19},{19,3},{4,20},{20... | collective-permute-start | bytes 5111816 | tf_op jit(solution)/shard_map/ppermute | solution.py:52
  120.2 5.8 %collective-permute-start.8 = (bf16[4,832,256]{2,1,0:T(8,128)(2,1)}, bf16[4,832,256]{2,1,0:T(8,128)(2,1)}, u32[]{:S(2)}, u32[]{:S(2)}) collective-permute-start(bf16[4,832,256]{2,1,0:T(8,128)(2,1)} %collective-permute-done.4.p2), channel_id=1, source_target_pairs={{0,16},{16,0},{1,17},{17,1},{2,18},{18,2},{3,19},{19,3},{4,20},{20... | collective-permute-start | bytes 5111816 | tf_op jit(solution)/shard_map/ppermute | solution.py:52
  122.1 6.3 %collective-permute-start.7 = (bf16[4,832,256]{2,1,0:T(8,128)(2,1)}, bf16[4,832,256]{2,1,0:T(8,128)(2,1)}, u32[]{:S(2)}, u32[]{:S(2)}) collective-permute-start(bf16[4,832,256]{2,1,0:T(8,128)(2,1)} %collective-permute-done.3.p1), channel_id=1, source_target_pairs={{0,16},{16,0},{1,17},{17,1},{2,18},{18,2},{3,19},{19,3},{4,20},{20... | collective-permute-start | bytes 5111816 | tf_op jit(solution)/shard_map/ppermute | solution.py:52
  128.5 1.4 copy-start.1
  151.3 4.2 %collective-permute-start.10 = (f32[4,16,8,384]{3,2,1,0:T(8,128)S(1)}, f32[4,16,8,384]{3,2,1,0:T(8,128)S(1)}, u32[]{:S(2)}, u32[]{:S(2)}) collective-permute-start(f32[4,16,8,384]{3,2,1,0:T(8,128)S(1)} %get-tuple-element.5), channel_id=1, source_target_pairs={{0,16},{16,0},{1,17},{17,1},{2,18},{18,2},{3,19},{19,3},{4,20},{20... | collective-permute-start | bytes 2359304 | tf_op jit(solution)/shard_map/ppermute | solution.py:52

commit v2 on v1

--- a/solution.py
+++ b/solution.py
@@ -60,7 +60,7 @@
     place, pol_hbm, ref_hbm, pol_gain, ref_gain, rows8,
     p0, p1, p2, p3, p4, p5, p6, p7,
     keep, give,
-    held, normed, acc, up, down, slopes, low_t, grad, hid, sems,
+    held, normed, acc, up, down, low_t, grad, hid, sems,
 ):
     x, y, c = place[0], place[1], place[2]
     parts = (p0, p1, p2, p3, p4, p5, p6, p7)
@@ -72,7 +72,6 @@
     for copy in first + copies:
         copy.start()
 
-    acc[...] = jnp.zeros_like(acc)
     step = 32
     for which, gain in ((0, pol_gain), (1, ref_gain)):
         first[which].wait()
@@ -83,47 +82,56 @@
             ms = jnp.sum(v * v, axis=-1, keepdims=True) * (1.0 / WIDTH)
             n = (v * lax.rsqrt(ms + NORM_EPS) * gain[...]).astype(bf16)
             for k in range(Y):
-                normed[which, k, at, :] = n[:, k * KY : (k + 1) * KY]
+                normed[k, pl.ds(pl.multiple_of(which * ROWS + i * step, step), step), :] = n[:, k * KY : (k + 1) * KY]
             return carry
 
         lax.fori_loop(0, ROWS // step, norm, 0)
 
-    for i in range(8):
-        copies[i].wait()
-        core = c if i < 4 else 1 - c
-        k2 = SHIFTS[i % 4]
-
-        def block(q, carry, i=i, core=core, k2=k2):
-            k1 = jnp.where(q == 2, 3, jnp.where(q == 3, 2, q))
-            kx = jnp.where(core == 0, k1, k2)
-            ky = jnp.where(core == 0, k2, k1)
-            xq = lax.rem(x + X - kx, X)
-            ys = lax.rem(y + Y - ky, Y)
+
+    def order(q):
+        return jnp.where(q == 2, 3, jnp.where(q == 3, 2, q))
+
+    for half in range(2):
+        core = c if half == 0 else 1 - c
+        for i in range(4):
+            copies[half * 4 + i].wait()
+
+        def column(s, carry, half=half, core=core):
+            xq = lax.rem(x + X - order(s), X)
             j = core * X + xq
-            w = held[i, q, 0:KY, :]
-            for which in range(2):
-                acc[which, j] += bdot(normed[which, ys], w, ((1,), (0,)))
             at = pl.ds(pl.multiple_of(xq * 16, 16), 16)
-            e = held[i, q, KY:PIECE, :]
-
-            @pl.when(core == 0)
-            def _():
-                for z in range(ZH):
-                    up[ys, at, z * TM : (z + 1) * TM] = e[z * 16 : (z + 1) * 16, 0:TM]
-
-            @pl.when(core == 1)
-            def _():
-                down[ys, at, :] = jnp.concatenate(
-                    [e[z * 16 : (z + 1) * 16, 0:KM] for z in range(ZH)], axis=1
-                )
+            ysn, blk = [], []
+            for n in range(4):
+                ysn.append(lax.rem(y + Y - SHIFTS[n], Y))
+                blk.append((half * 4 + jnp.where(core == 0, n, s), jnp.where(core == 0, s, n)))
+            total = None
+            for n in range(4):
+                part = bdot(normed[ysn[n]], held[blk[n][0], blk[n][1], 0:KY, :], ((1,), (0,)))
+                total = part if total is None else total + part
+            acc[j] = total
+
+            for n in range(4):
+                ys = ysn[n]
+                e = held[blk[n][0], blk[n][1], KY:PIECE, :]
+
+                @pl.when(core == 0)
+                def _(ys=ys, e=e):
+                    for z in range(ZH):
+                        up[ys, at, z * TM : (z + 1) * TM] = e[z * 16 : (z + 1) * 16, 0:TM]
+
+                @pl.when(core == 1)
+                def _(ys=ys, e=e):
+                    down[ys, at, :] = jnp.concatenate(
+                        [e[z * 16 : (z + 1) * 16, 0:KM] for z in range(ZH)], axis=1
+                    )
 
             return carry
 
-        lax.fori_loop(0, 4, block, 0)
+        lax.fori_loop(0, 4, column, 0)
 
     low = jnp.zeros((ROWS, RANK), f32)
     for k in range(Y):
-        low += bdot(normed[0, k], down[k], ((1,), (1,)))
+        low += bdot(normed[k, 0:ROWS], down[k], ((1,), (1,)))
     low16 = low.astype(bf16)
     low_t[...] = low.T.astype(bf16)
 
@@ -139,41 +147,41 @@
     s_ref = jnp.zeros((ROWS, 1), f32)
     hit = jnp.zeros((ROWS, 1), f32)
     for j in range(8):
-        v = acc[0, j] + bdot(low16, up_part(j), ((1,), (0,)))
-        acc[0, j] = v
+        v = acc[j, 0:ROWS] + bdot(low16, up_part(j), ((1,), (0,)))
+        acc[j, 0:ROWS] = v
         s_pol += jnp.sum(jnp.exp(v), axis=-1, keepdims=True)
         hit += jnp.sum(jnp.where(iota == acts - j * NB, v, 0.0), axis=-1, keepdims=True)
-        s_ref += jnp.sum(jnp.exp(acc[1, j]), axis=-1, keepdims=True)
+        s_ref += jnp.sum(jnp.exp(acc[j, ROWS:]), axis=-1, keepdims=True)
     lse_pol, lse_ref = jnp.log(s_pol), jnp.log(s_ref)
     taken = hit - lse_pol
     t = jnp.tanh((taken - old) / CLIP_LOG)
     pull = mask * (adv * jnp.exp(CLIP_LOG * t) * (1.0 - t * t))
     div = jnp.zeros((ROWS, 1), f32)
     for j in range(8):
-        logp = acc[0, j] - lse_pol
-        gap = logp - (acc[1, j] - lse_ref).astype(bf16).astype(f32)
+        logp = acc[j, 0:ROWS] - lse_pol
+        gap = logp - (acc[j, ROWS:] - lse_ref).astype(bf16).astype(f32)
         p = jnp.exp(logp)
         div += jnp.sum(p * gap, axis=-1, keepdims=True)
-        acc[0, j] = p
-        acc[1, j] = gap
+        acc[j, 0:ROWS] = p
+        acc[j, ROWS:] = gap
     scale = mask * KL_COEF
     base = pull - scale * div
     low_slopes = jnp.zeros((ROWS, RANK), f32)
     for j in range(8):
-        s = acc[0, j] * (scale * acc[1, j] + base) - jnp.where(iota == acts - j * NB, pull, 0.0)
+        s = acc[j, 0:ROWS] * (scale * acc[j, ROWS:] + base) - jnp.where(iota == acts - j * NB, pull, 0.0)
         s16 = s.astype(bf16)
         grad[:, j * NB : (j + 1) * NB] = bdot(low_t[...], s16, ((1,), (0,)))
         low_slopes += bdot(s16, up_part(j), ((1,), (1,)))
     low_slopes_t = low_slopes.T.astype(bf16)
     for k in range(Y):
-        grad[:, TOKENS + k * KY : TOKENS + (k + 1) * KY] = bdot(low_slopes_t, normed[0, k], ((1,), (0,)))
+        grad[:, TOKENS + k * KY : TOKENS + (k + 1) * KY] = bdot(low_slopes_t, normed[k, 0:ROWS], ((1,), (0,)))
 
     blank = jnp.zeros((8, LANES - TM - KM), f32)
     for out, core in ((keep, c), (give, 1 - c)):
         for xx in range(X):
             at = pl.ds(pl.multiple_of((xx * C + core) * 8, 8), 8)
             for m in range(Y * ZH):
-                out[xx, m] = jnp.concatenate(
+                sums = jnp.concatenate(
                     [
                         grad[at, m * TM : (m + 1) * TM],
                         grad[at, TOKENS + m * KM : TOKENS + (m + 1) * KM],
@@ -181,6 +189,7 @@
                     ],
                     axis=1,
                 )
+                out[xx, m] = sums.astype(out.dtype)
 
 
 def local(ref_hidden, pol_hidden, ref_gain, pol_gain, head, down_w, up_w, actions, present, old, adv):
@@ -200,13 +209,15 @@
     own = [four] + [shift_second(four, k) for k in SHIFTS[1:]]
     other = [swap_cores(v) for v in own]
 
+    ref_hidden, guard = lax.optimization_barrier((ref_hidden, swap_cores(mine[:16, :NB])))
     ref_rows = lax.all_to_all(
         ref_hidden.reshape(Y * ZH, ROWS // (Y * ZH), WIDTH), ("y", "zh"), 0, 0, tiled=True
     ).reshape(ROWS, WIDTH)
     pol_rows = pol_hidden.reshape(ROWS, WIDTH)
     rows8 = jnp.stack(
         [v.reshape(ROWS).astype(f32) for v in (actions, present, old, adv)]
-        + [jnp.zeros((ROWS,), f32)] * 4
+        + [jnp.zeros((ROWS,), f32)] * 3
+        + [guard[0].astype(f32)]
     )
     place = jnp.stack([x, y, c]).astype(jnp.int32)
 
@@ -215,16 +226,15 @@
     out = jax.ShapeDtypeStruct((X, Y * ZH, 8, LANES), f32)
     keep, give = pl.pallas_call(
         kernel,
-        out_shape=(out, out),
+        out_shape=(out, jax.ShapeDtypeStruct(out.shape, bf16)),
         in_specs=[pl.BlockSpec(memory_space=pltpu.SMEM), hbm, hbm, vmem, vmem, vmem] + [hbm] * 8,
         out_specs=(vmem, vmem),
         scratch_shapes=[
             pltpu.VMEM((8, 4, PIECE, NB), bf16),
-            pltpu.VMEM((2, Y, ROWS, KY), bf16),
-            pltpu.VMEM((2, C * X, ROWS, NB), f32),
+            pltpu.VMEM((Y, 2 * ROWS, KY), bf16),
+            pltpu.VMEM((C * X, 2 * ROWS, NB), f32),
             pltpu.VMEM((Y, RANK, TOKENS // Y), bf16),
             pltpu.VMEM((Y, RANK, KY), bf16),
-            pltpu.VMEM((8, 128), bf16),
             pltpu.VMEM((RANK, ROWS), bf16),
             pltpu.VMEM((RANK, TOKENS + WIDTH), f32),
             pltpu.VMEM((2, ROWS, WIDTH), bf16),
@@ -239,10 +249,11 @@
         pol_gain.reshape(1, WIDTH), ref_gain.reshape(1, WIDTH), rows8, *own, *other,
     )
 
-    part = keep + swap_cores(give)
-    part = lax.all_to_all(part.reshape(X * Y, ZH, 8, LANES), ("x", "y"), 0, 0, tiled=True).sum(0)
+    part = (keep + swap_cores(give).astype(f32)).astype(bf16)
+    part = lax.all_to_all(part.reshape(X * Y, ZH, 8, LANES), ("x", "y"), 0, 0, tiled=True)
+    part = part.astype(f32).sum(0).astype(bf16)
     part = jnp.broadcast_to(part[None], (ZL, ZH, 8, LANES)).reshape(ZL * ZH, 8, LANES)
-    part = lax.all_to_all(part, ("zl", "zh"), 0, 0, tiled=True).sum(0)
+    part = lax.all_to_all(part, ("zl", "zh"), 0, 0, tiled=True).astype(f32).sum(0)
     whole = lax.all_to_all(
         jnp.broadcast_to(part[None], (X * C, 8, LANES)), ("x", "c"), 0, 0, tiled=True
     ).reshape(RANK, LANES)

time: 228 us -> 211 us (0.925)
  blocking collectives: 107 us -> 85.9 us
  starting transfers between devices: 40.6 us -> 59.9 us
  waiting for transfers between devices: 51 us -> 40.1 us
  Pallas kernels: 21.4 us -> 17.6 us
    ppermute x5 -> x6, starting transfers between devices: 11.2 us -> 28.9 us  [swap_cores(): return lax.ppermute(v, 'c', [(0, 1), (1, 0)])]
    all_to_all x1, blocking collectives: 40 us -> 25.8 us  [local(): lax.all_to_all(part, ('zl', 'zh'), 0, 0, tiled=True).astype(f32).sum(0)]
    ppermute x3, waiting for transfers between devices: 17.8 us -> 11.7 us  [shift_first(): lax.ppermute(v, ('x', 'c', 'y'), pairs(lambda x, c, y: (x + k * (c == 0),...]
    all_to_all x1, blocking collectives: 17.9 us -> 12.4 us  [local(): lax.all_to_all(part.reshape(X * Y, ZH, 8, LANES), ('x', 'y'), 0, 0, tiled...]
    ppermute x3, waiting for transfers between devices: 28 us -> 23.1 us  [shift_second(): lax.ppermute(v, ('x', 'c', 'y'), pairs(lambda x, c, y: (x + k * (c == 1),...]
    pallas_call x1, Pallas kernels: 21.4 us -> 17.6 us  [local(): pl.pallas_call(kernel, out_shape=(out, jax.ShapeDtypeStruct(out.shape, bf...]
    ppermute x5 -> x6, waiting for transfers between devices: 5.19 us -> 5.31 us  [swap_cores(): return lax.ppermute(v, 'c', [(0, 1), (1, 0)])]
  transfers between devices with their start and end apart: 12 -> 13, of which waited for: 8 -> 8; matrix products, arithmetic and copies ran while one was open for 0% -> 1% of each run, Pallas kernels for 0% -> 0%
where the time goes in v2:
time: 211 us; the launch traced here: 210 us
  blocking collectives  85.9 us (41%)
  starting transfers between devices  59.9 us (28%)
  waiting for transfers between devices  40.1 us (19%)
  Pallas kernels  17.6 us (8%)
  local copies, waits for them, and re-layouts  4.59 us (2%)
    all_to_all x1, blocking collectives, local(): lax.all_to_all(jnp.broadcast_to(piece[None], (ZH, KM + 16, NB)), 'zh', 0,...  37.1 us
    ppermute x6, starting transfers between devices, swap_cores(): return lax.ppermute(v, 'c', [(0, 1), (1, 0)])  28.9 us
    all_to_all x1, blocking collectives, local(): lax.all_to_all(part, ('zl', 'zh'), 0, 0, tiled=True).astype(f32).sum(0)  25.8 us
    ppermute x3, waiting for transfers between devices, shift_second(): lax.ppermute(v, ('x', 'c', 'y'), pairs(lambda x, c, y: (x + k * (c == 1),...  23.1 us
    pallas_call x1, Pallas kernels, local(): pl.pallas_call(kernel, out_shape=(out, jax.ShapeDtypeStruct(out.shape, bf...  17.6 us
    all_to_all x1, blocking collectives, local(): lax.all_to_all(part.reshape(X * Y, ZH, 8, LANES), ('x', 'y'), 0, 0, tiled...  12.4 us
    ppermute x3, waiting for transfers between devices, shift_first(): lax.ppermute(v, ('x', 'c', 'y'), pairs(lambda x, c, y: (x + k * (c == 0),...  11.7 us
    all_to_all x1, starting transfers between devices, local(): lax.all_to_all(ref_hidden.reshape(Y * ZH, ROWS // (Y * ZH), WIDTH), ('y',...  11.1 us
  transfers between devices with their start and end apart: 13, of which 8 were waited for; matrix products, arithmetic and copies ran while one was open for 1% of the time, Pallas kernels for 0%

profile of v2, /device:TPU:1, one launch (start us, length us, event | category | flops | bytes accessed | tf_op | source)
XLA Modules:
  0.0 210.2 jit_solution(8922199986301217880)
XLA Ops:
  0.7 1.1 copy-done
  1.8 0.7 fusion
  2.6 37.1 %all_to_all.25 = bf16[4,208,256]{2,1,0:T(8,128)(2,1)S(1)} all-to-all(bf16[4,208,256]{2,1,0:T(8,128)(2,1)S(1)} %broadcast_in_dim.6), channel_id=1, replica_groups=mesh['x'=4,'zl'=4,'c'=2,'y'=4,'zh'=4] {'zh'}, dimensions={0} | all-to-all | bytes 851968 | tf_op jit(solution)/shard_map/all_to_all | solution.py:202
  39.7 3.7 %collective-permute-start = (bf16[16,256]{1,0:T(8,128)(2,1)S(1)}, bf16[16,256]{1,0:T(8,128)(2,1)S(1)}, u32[]{:S(2)}, u32[]{:S(2)}) collective-permute-start(bf16[16,256]{1,0:T(8,128)(2,1)S(1)} %slice.25), channel_id=1, source_target_pairs={{0,16},{16,0},{1,17},{17,1},{2,18},{18,2},{3,19},{19,3},{4,20},{20... | collective-permute-start | bytes 24584 | tf_op jit(solution)/shard_map/ppermute | solution.py:52
  43.5 0.8 collective-permute-done
  44.3 11.1 %all-to-all-start.1 = ((bf16[16,16,3072]{2,1,0:T(8,128)(2,1)}), bf16[16,16,3072]{2,1,0:T(8,128)(2,1)}, u32[]{:S(2)}, u32[]{:S(2)}) async-start(bf16[16,16,3072]{2,1,0:T(8,128)(2,1)} %bitcast.7), calls=%async_computation.1 | async-start | bytes 3145728 | tf_op jit(solution)/shard_map/all_to_all | solution.py:213
  55.5 4.4 %collective-permute-start.2 = (bf16[832,256]{1,0:T(8,128)(2,1)S(1)}, bf16[832,256]{1,0:T(8,128)(2,1)S(1)}, u32[]{:S(2)}, u32[]{:S(2)}) collective-permute-start(bf16[832,256]{1,0:T(8,128)(2,1)S(1)} %get-tuple-element.11), channel_id=1, source_target_pairs={{0,384},{4,388},{8,392},{12,396},{16,28},{20,16},{24,20},{28,24},{... | collective-permute-start | bytes 1277960 | tf_op jit(solution)/shard_map/ppermute | solution.py:44
  59.9 1.9 collective-permute-start.1
  61.8 3.7 %collective-permute-start.3 = (bf16[832,256]{1,0:T(8,128)(2,1)S(1)}, bf16[832,256]{1,0:T(8,128)(2,1)S(1)}, u32[]{:S(2)}, u32[]{:S(2)}) collective-permute-start(bf16[832,256]{1,0:T(8,128)(2,1)S(1)} %get-tuple-element.11), channel_id=1, source_target_pairs={{0,256},{4,260},{8,264},{12,268},{16,24},{20,28},{24,16},{28,20},{... | collective-permute-start | bytes 1277960 | tf_op jit(solution)/shard_map/ppermute | solution.py:44
  65.5 1.6 collective-permute-done.2
  67.1 10.1 %collective-permute-done.1 = bf16[832,256]{1,0:T(8,128)(2,1)S(1)} collective-permute-done((bf16[832,256]{1,0:T(8,128)(2,1)S(1)}, bf16[832,256]{1,0:T(8,128)(2,1)S(1)}, u32[]{:S(2)}, u32[]{:S(2)}) %collective-permute-start.1) | collective-permute-done | bytes 426016 | tf_op jit(solution)/shard_map/ppermute | solution.py:44
  77.3 0.2 pad_maximum_fusion.p0
  77.5 4.7 %collective-permute-start.6 = (bf16[4,832,256]{2,1,0:T(8,128)(2,1)S(1)}, bf16[4,832,256]{2,1,0:T(8,128)(2,1)}, u32[]{:S(2)}, u32[]{:S(2)}) collective-permute-start(bf16[4,832,256]{2,1,0:T(8,128)(2,1)S(1)} %pad_maximum_fusion.p0), channel_id=1, source_target_pairs={{0,8},{4,12},{8,0},{12,4},{16,272},{20,276},{24,280},{28,284},{128... | collective-permute-start | bytes 5111816 | tf_op jit(solution)/shard_map/ppermute | solution.py:48
  82.1 2.8 %collective-permute-start.5 = (bf16[4,832,256]{2,1,0:T(8,128)(2,1)S(1)}, bf16[4,832,256]{2,1,0:T(8,128)(2,1)}, u32[]{:S(2)}, u32[]{:S(2)}) collective-permute-start(bf16[4,832,256]{2,1,0:T(8,128)(2,1)S(1)} %pad_maximum_fusion.p0), channel_id=1, source_target_pairs={{0,12},{4,0},{8,4},{12,8},{16,400},{20,404},{24,408},{28,412},{128... | collective-permute-start | bytes 5111816 | tf_op jit(solution)/shard_map/ppermute | solution.py:48
  84.9 2.5 %collective-permute-start.4 = (bf16[4,832,256]{2,1,0:T(8,128)(2,1)S(1)}, bf16[4,832,256]{2,1,0:T(8,128)(2,1)}, u32[]{:S(2)}, u32[]{:S(2)}) collective-permute-start(bf16[4,832,256]{2,1,0:T(8,128)(2,1)S(1)} %pad_maximum_fusion.p0), channel_id=1, source_target_pairs={{0,4},{4,8},{8,12},{12,0},{16,144},{20,148},{24,152},{28,156},{128... | collective-permute-start | bytes 5111816 | tf_op jit(solution)/shard_map/ppermute | solution.py:48
  87.4 2.5 %collective-permute-start.7 = (bf16[4,832,256]{2,1,0:T(8,128)(2,1)S(1)}, bf16[4,832,256]{2,1,0:T(8,128)(2,1)}, u32[]{:S(2)}, u32[]{:S(2)}) collective-permute-start(bf16[4,832,256]{2,1,0:T(8,128)(2,1)S(1)} %pad_maximum_fusion.p0), channel_id=1, source_target_pairs={{0,16},{16,0},{1,17},{17,1},{2,18},{18,2},{3,19},{19,3},{4,20},{20... | collective-permute-start | bytes 5111816 | tf_op jit(solution)/shard_map/ppermute | solution.py:52
  89.9 12.1 %collective-permute-done.6.p3 = bf16[4,832,256]{2,1,0:T(8,128)(2,1)} collective-permute-done((bf16[4,832,256]{2,1,0:T(8,128)(2,1)S(1)}, bf16[4,832,256]{2,1,0:T(8,128)(2,1)}, u32[]{:S(2)}, u32[]{:S(2)}) %collective-permute-start.6) | collective-permute-done | bytes 1703968 | tf_op jit(solution)/shard_map/ppermute | solution.py:48
  102.0 7.3 %collective-permute-start.10 = (bf16[4,832,256]{2,1,0:T(8,128)(2,1)}, bf16[4,832,256]{2,1,0:T(8,128)(2,1)}, u32[]{:S(2)}, u32[]{:S(2)}) collective-permute-start(bf16[4,832,256]{2,1,0:T(8,128)(2,1)} %collective-permute-done.6.p3), channel_id=1, source_target_pairs={{0,16},{16,0},{1,17},{17,1},{2,18},{18,2},{3,19},{19,3},{4,20},{20... | collective-permute-start | bytes 5111816 | tf_op jit(solution)/shard_map/ppermute | solution.py:52
  109.3 11.0 %collective-permute-done.5.p2 = bf16[4,832,256]{2,1,0:T(8,128)(2,1)} collective-permute-done((bf16[4,832,256]{2,1,0:T(8,128)(2,1)S(1)}, bf16[4,832,256]{2,1,0:T(8,128)(2,1)}, u32[]{:S(2)}, u32[]{:S(2)}) %collective-permute-start.5) | collective-permute-done | bytes 1703968 | tf_op jit(solution)/shard_map/ppermute | solution.py:48
  120.3 11.1 %collective-permute-start.9 = (bf16[4,832,256]{2,1,0:T(8,128)(2,1)}, bf16[4,832,256]{2,1,0:T(8,128)(2,1)}, u32[]{:S(2)}, u32[]{:S(2)}) collective-permute-start(bf16[4,832,256]{2,1,0:T(8,128)(2,1)} %collective-permute-done.5.p2), channel_id=1, source_target_pairs={{0,16},{16,0},{1,17},{17,1},{2,18},{18,2},{3,19},{19,3},{4,20},{20... | collective-permute-start | bytes 5111816 | tf_op jit(solution)/shard_map/ppermute | solution.py:52
  131.5 1.9 collective-permute-start.8
  134.3 0.7 collective-permute-done.9.p6
  135.0 2.4 %collective-permute-done.8.p5 = bf16[4,832,256]{2,1,0:T(8,128)(2,1)} collective-permute-done((bf16[4,832,256]{2,1,0:T(8,128)(2,1)}, bf16[4,832,256]{2,1,0:T(8,128)(2,1)}, u32[]{:S(2)}, u32[]{:S(2)}) %collective-permute-start.8) | collective-permute-done | bytes 1703968 | tf_op jit(solution)/shard_map/ppermute | solution.py:52
  137.4 1.4 copy-done.1
  138.8 17.6 %shard_map.122 = (f32[4,16,8,384]{3,2,1,0:T(8,128)S(1)}, bf16[4,16,8,384]{3,2,1,0:T(8,128)(2,1)S(1)}) custom-call(s32[3]{0:T(128)S(1)} %pad_add_fusion.place, bf16[256,3072]{1,0:T(8,128)(2,1)S(1)} %bitcast.24, bf16[256,3072]{1,0:T(8,128)(2,1)} %bitcast.8.ref_hbm, f32[1,3072]{1,0:T(1,128)S(1)} %bitcast.25, f32[1,3072]{1,0:T(1,128)S(1)} %bitcast.26, ...), custom_call_target="tpu_custom_call" | custom-call | flops 6442450944 | bytes 18874368 | tf_op jit(solution)/shard_map/pallas_call | solution.py:227
  156.4 2.3 %collective-permute-start.11 = (bf16[4,16,8,384]{3,2,1,0:T(8,128)(2,1)S(1)}, bf16[4,16,8,384]{3,2,1,0:T(8,128)(2,1)S(1)}, u32[]{:S(2)}, u32[]{:S(2)}) collective-permute-start(bf16[4,16,8,384]{3,2,1,0:T(8,128)(2,1)S(1)} %get-tuple-element.9), channel_id=1, source_target_pairs={{0,16},{16,0},{1,17},{17,1},{2,18},{18,2},{3,19},{19,3},{4,20},{20... | collective-permute-start | bytes 1179656 | tf_op jit(solution)/shard_map/ppermute | solution.py:52
  158.7 1.3 collective-permute-done.11
  160.1 12.4 %all_to_all.26 = bf16[16,4,8,384]{3,2,1,0:T(8,128)(2,1)S(1)} all-to-all(bf16[16,4,8,384]{3,2,1,0:T(8,128)(2,1)S(1)} %bitcast.29), channel_id=1, replica_groups=mesh['x'=4,'zl'=4,'c'=2,'y'=4,'zh'=4] {'x','y'}, dimensions={0} | all-to-all | bytes 786432 | tf_op jit(solution)/shard_map/all_to_all | solution.py:253
  172.7 25.8 %all_to_all.27 = bf16[16,8,384]{2,1,0:T(8,128)(2,1)S(1)} all-to-all(bf16[16,8,384]{2,1,0:T(8,128)(2,1)S(1)} %bitcast.35), channel_id=1, replica_groups=mesh['x'=4,'zl'=4,'c'=2,'y'=4,'zh'=4] {'zl','zh'}, dimensions={0} | all-to-all | bytes 196608 | tf_op jit(solution)/shard_map/all_to_all | solution.py:256
  198.5 10.5 %all_to_all.28 = f32[8,8,384]{2,1,0:T(8,128)S(1)} all-to-all(f32[8,8,384]{2,1,0:T(8,128)S(1)} %broadcast_in_dim.8), channel_id=1, replica_groups=mesh['x'=4,'zl'=4,'c'=2,'y'=4,'zh'=4] {'x','c'}, dimensions={0} | all-to-all | bytes 196608 | tf_op jit(solution)/shard_map/all_to_all | solution.py:257
  209.0 0.6 slice_bitcast_fusion.1
  209.6 0.6 slice_bitcast_fusion
  (46 shorter events, 1.2 us)
Async XLA Ops:
  0.6 1.1 copy-start
  39.7 4.6 %collective-permute-start = (bf16[16,256]{1,0:T(8,128)(2,1)S(1)}, bf16[16,256]{1,0:T(8,128)(2,1)S(1)}, u32[]{:S(2)}, u32[]{:S(2)}) collective-permute-start(bf16[16,256]{1,0:T(8,128)(2,1)S(1)} %slice.25), channel_id=1, source_target_pairs={{0,16},{16,0},{1,17},{17,1},{2,18},{18,2},{3,19},{19,3},{4,20},{20... | collective-permute-start | bytes 24584 | tf_op jit(solution)/shard_map/ppermute | solution.py:52
  44.3 93.1 %all-to-all-start.1 = ((bf16[16,16,3072]{2,1,0:T(8,128)(2,1)}), bf16[16,16,3072]{2,1,0:T(8,128)(2,1)}, u32[]{:S(2)}, u32[]{:S(2)}) async-start(bf16[16,16,3072]{2,1,0:T(8,128)(2,1)} %bitcast.7), calls=%async_computation.1 | async-start | bytes 3145728 | tf_op jit(solution)/shard_map/all_to_all | solution.py:213
  55.5 11.6 %collective-permute-start.2 = (bf16[832,256]{1,0:T(8,128)(2,1)S(1)}, bf16[832,256]{1,0:T(8,128)(2,1)S(1)}, u32[]{:S(2)}, u32[]{:S(2)}) collective-permute-start(bf16[832,256]{1,0:T(8,128)(2,1)S(1)} %get-tuple-element.11), channel_id=1, source_target_pairs={{0,384},{4,388},{8,392},{12,396},{16,28},{20,16},{24,20},{28,24},{... | collective-permute-start | bytes 1277960 | tf_op jit(solution)/shard_map/ppermute | solution.py:44
  59.9 17.3 %collective-permute-start.1 = (bf16[832,256]{1,0:T(8,128)(2,1)S(1)}, bf16[832,256]{1,0:T(8,128)(2,1)S(1)}, u32[]{:S(2)}, u32[]{:S(2)}) collective-permute-start(bf16[832,256]{1,0:T(8,128)(2,1)S(1)} %get-tuple-element.11), channel_id=1, source_target_pairs={{0,128},{4,132},{8,136},{12,140},{16,20},{20,24},{24,28},{28,16},{... | collective-permute-start | bytes 1277960 | tf_op jit(solution)/shard_map/ppermute | solution.py:44
  61.8 15.4 %collective-permute-start.3 = (bf16[832,256]{1,0:T(8,128)(2,1)S(1)}, bf16[832,256]{1,0:T(8,128)(2,1)S(1)}, u32[]{:S(2)}, u32[]{:S(2)}) collective-permute-start(bf16[832,256]{1,0:T(8,128)(2,1)S(1)} %get-tuple-element.11), channel_id=1, source_target_pairs={{0,256},{4,260},{8,264},{12,268},{16,24},{20,28},{24,16},{28,20},{... | collective-permute-start | bytes 1277960 | tf_op jit(solution)/shard_map/ppermute | solution.py:44
  77.2 56.2 %copy-start.6 = (s32[1,32,8]{1,2,0:T(8,128)S(1)}, s32[1,32,8]{1,2,0:T(8,128)}, u32[]{:S(2)}) copy-start(s32[1,32,8]{1,2,0:T(8,128)} %param.18) | copy-start | bytes 3076
  77.2 56.2 %copy-start.7 = (s32[1,32,8]{1,2,0:T(8,128)S(1)}, s32[1,32,8]{1,2,0:T(8,128)}, u32[]{:S(2)}) copy-start(s32[1,32,8]{1,2,0:T(8,128)} %param.19) | copy-start | bytes 3076
  77.2 56.6 %copy-start.4 = (f32[1,32,8]{1,2,0:T(8,128)S(1)}, f32[1,32,8]{1,2,0:T(8,128)}, u32[]{:S(2)}) copy-start(f32[1,32,8]{1,2,0:T(8,128)} %param.20) | copy-start | bytes 3076
  77.2 56.7 %copy-start.5 = (f32[1,32,8]{1,2,0:T(8,128)S(1)}, f32[1,32,8]{1,2,0:T(8,128)}, u32[]{:S(2)}) copy-start(f32[1,32,8]{1,2,0:T(8,128)} %param.21) | copy-start | bytes 3076
  77.2 60.2 %copy-start.2 = (f32[3072]{0:T(1024)S(1)}, f32[3072]{0:T(1024)}, u32[]{:S(2)}) copy-start(f32[3072]{0:T(1024)} %param.14) | copy-start | bytes 36868
  77.2 60.2 %copy-start.3 = (f32[3072]{0:T(1024)S(1)}, f32[3072]{0:T(1024)}, u32[]{:S(2)}) copy-start(f32[3072]{0:T(1024)} %param.13) | copy-start | bytes 36868
  77.5 24.5 %collective-permute-start.6 = (bf16[4,832,256]{2,1,0:T(8,128)(2,1)S(1)}, bf16[4,832,256]{2,1,0:T(8,128)(2,1)}, u32[]{:S(2)}, u32[]{:S(2)}) collective-permute-start(bf16[4,832,256]{2,1,0:T(8,128)(2,1)S(1)} %pad_maximum_fusion.p0), channel_id=1, source_target_pairs={{0,8},{4,12},{8,0},{12,4},{16,272},{20,276},{24,280},{28,284},{128... | collective-permute-start | bytes 5111816 | tf_op jit(solution)/shard_map/ppermute | solution.py:48
  82.1 38.2 %collective-permute-start.5 = (bf16[4,832,256]{2,1,0:T(8,128)(2,1)S(1)}, bf16[4,832,256]{2,1,0:T(8,128)(2,1)}, u32[]{:S(2)}, u32[]{:S(2)}) collective-permute-start(bf16[4,832,256]{2,1,0:T(8,128)(2,1)S(1)} %pad_maximum_fusion.p0), channel_id=1, source_target_pairs={{0,12},{4,0},{8,4},{12,8},{16,400},{20,404},{24,408},{28,412},{128... | collective-permute-start | bytes 5111816 | tf_op jit(solution)/shard_map/ppermute | solution.py:48
  84.9 46.5 %collective-permute-start.4 = (bf16[4,832,256]{2,1,0:T(8,128)(2,1)S(1)}, bf16[4,832,256]{2,1,0:T(8,128)(2,1)}, u32[]{:S(2)}, u32[]{:S(2)}) collective-permute-start(bf16[4,832,256]{2,1,0:T(8,128)(2,1)S(1)} %pad_maximum_fusion.p0), channel_id=1, source_target_pairs={{0,4},{4,8},{8,12},{12,0},{16,144},{20,148},{24,152},{28,156},{128... | collective-permute-start | bytes 5111816 | tf_op jit(solution)/shard_map/ppermute | solution.py:48
  87.4 46.8 %collective-permute-start.7 = (bf16[4,832,256]{2,1,0:T(8,128)(2,1)S(1)}, bf16[4,832,256]{2,1,0:T(8,128)(2,1)}, u32[]{:S(2)}, u32[]{:S(2)}) collective-permute-start(bf16[4,832,256]{2,1,0:T(8,128)(2,1)S(1)} %pad_maximum_fusion.p0), channel_id=1, source_target_pairs={{0,16},{16,0},{1,17},{17,1},{2,18},{18,2},{3,19},{19,3},{4,20},{20... | collective-permute-start | bytes 5111816 | tf_op jit(solution)/shard_map/ppermute | solution.py:52
  102.0 32.3 %collective-permute-start.10 = (bf16[4,832,256]{2,1,0:T(8,128)(2,1)}, bf16[4,832,256]{2,1,0:T(8,128)(2,1)}, u32[]{:S(2)}, u32[]{:S(2)}) collective-permute-start(bf16[4,832,256]{2,1,0:T(8,128)(2,1)} %collective-permute-done.6.p3), channel_id=1, source_target_pairs={{0,16},{16,0},{1,17},{17,1},{2,18},{18,2},{3,19},{19,3},{4,20},{20... | collective-permute-start | bytes 5111816 | tf_op jit(solution)/shard_map/ppermute | solution.py:52
  120.3 14.7 %collective-permute-start.9 = (bf16[4,832,256]{2,1,0:T(8,128)(2,1)}, bf16[4,832,256]{2,1,0:T(8,128)(2,1)}, u32[]{:S(2)}, u32[]{:S(2)}) collective-permute-start(bf16[4,832,256]{2,1,0:T(8,128)(2,1)} %collective-permute-done.5.p2), channel_id=1, source_target_pairs={{0,16},{16,0},{1,17},{17,1},{2,18},{18,2},{3,19},{19,3},{4,20},{20... | collective-permute-start | bytes 5111816 | tf_op jit(solution)/shard_map/ppermute | solution.py:52
  131.5 6.0 %collective-permute-start.8 = (bf16[4,832,256]{2,1,0:T(8,128)(2,1)}, bf16[4,832,256]{2,1,0:T(8,128)(2,1)}, u32[]{:S(2)}, u32[]{:S(2)}) collective-permute-start(bf16[4,832,256]{2,1,0:T(8,128)(2,1)} %collective-permute-done.4.p1), channel_id=1, source_target_pairs={{0,16},{16,0},{1,17},{17,1},{2,18},{18,2},{3,19},{19,3},{4,20},{20... | collective-permute-start | bytes 5111816 | tf_op jit(solution)/shard_map/ppermute | solution.py:52
  137.4 1.4 copy-start.1
  156.4 3.6 %collective-permute-start.11 = (bf16[4,16,8,384]{3,2,1,0:T(8,128)(2,1)S(1)}, bf16[4,16,8,384]{3,2,1,0:T(8,128)(2,1)S(1)}, u32[]{:S(2)}, u32[]{:S(2)}) collective-permute-start(bf16[4,16,8,384]{3,2,1,0:T(8,128)(2,1)S(1)} %get-tuple-element.9), channel_id=1, source_target_pairs={{0,16},{16,0},{1,17},{17,1},{2,18},{18,2},{3,19},{19,3},{4,20},{20... | collective-permute-start | bytes 1179656 | tf_op jit(solution)/shard_map/ppermute | solution.py:52

commit v3 on v2

--- a/solution.py
+++ b/solution.py
@@ -56,82 +56,122 @@
     return lax.dot_general(a, b, (dims, ((), ())), preferred_element_type=f32)
 
 
+def normalize(hid, gain, normed, offset):
+    step = 32
+
+    def norm(i, carry):
+        v = hid[pl.ds(pl.multiple_of(i * step, step), step), :].astype(f32)
+        ms = jnp.sum(v * v, axis=-1, keepdims=True) * (1.0 / WIDTH)
+        n = (v * lax.rsqrt(ms + NORM_EPS) * gain[...]).astype(bf16)
+        normed[pl.ds(pl.multiple_of(offset + i * step, step), step), :] = n
+        return carry
+
+    lax.fori_loop(0, ROWS // step, norm, 0, unroll=2)
+
+
+def policy_kernel(hid, gain, normed):
+    normalize(hid, gain, normed, 0)
+
+
+def fold(v):
+    return v[:, 0:128] + v[:, 128:256]
+
+
+def total_of(v):
+    return jnp.sum(v, axis=-1, keepdims=True)
+
+
 def kernel(
-    place, pol_hbm, ref_hbm, pol_gain, ref_gain, rows8,
+    place, pol_hbm, ref_hbm, ref_gain, rows8,
     p0, p1, p2, p3, p4, p5, p6, p7,
     keep, give,
-    held, normed, acc, up, down, low_t, grad, hid, sems,
+    held, extra, normed, acc, up, down, low_t, grad, hid, sems, extra_sems,
 ):
     x, y, c = place[0], place[1], place[2]
     parts = (p0, p1, p2, p3, p4, p5, p6, p7)
-    first = [
-        pltpu.make_async_copy(pol_hbm, hid.at[0], sems.at[8]),
-        pltpu.make_async_copy(ref_hbm, hid.at[1], sems.at[9]),
+    rows = pltpu.make_async_copy(ref_hbm, hid, sems.at[8])
+    policy = pltpu.make_async_copy(pol_hbm, normed.at[pl.ds(0, ROWS)], sems.at[9])
+    rows.start()
+    policy.start()
+
+    def place_of(i, q):
+        core = c if i < 4 else 1 - c
+        k1, k2 = SHIFTS[q], SHIFTS[i % 4]
+        kx = jnp.where(core == 0, k1, k2)
+        ky = jnp.where(core == 0, k2, k1)
+        return core, lax.rem(x + X - kx, X), lax.rem(y + Y - ky, Y)
+
+    def fetch(i, q):
+        core, xq, ys = place_of(i, q)
+        j = core * X + xq
+        pltpu.make_async_copy(
+            parts[i].at[q, pl.ds(0, KY)],
+            held.at[j, pl.ds(pl.multiple_of(ys * KY, KY), KY)],
+            sems.at[j],
+        ).start()
+
+    for half in range(2):
+        for step in range(4):
+
+            @pl.when(place_of(half * 4, 0)[0] == 0)
+            def _(half=half, step=step):
+                for n in range(4):
+                    fetch(half * 4 + n, step)
+
+            @pl.when(place_of(half * 4, 0)[0] == 1)
+            def _(half=half, step=step):
+                for n in range(4):
+                    fetch(half * 4 + step, n)
+
+    factors = [
+        pltpu.make_async_copy(parts[i].at[:, pl.ds(KY, ZH * 16)], extra.at[i], extra_sems.at[i])
+        for i in range(8)
     ]
-    copies = [pltpu.make_async_copy(parts[i], held.at[i], sems.at[i]) for i in range(8)]
-    for copy in first + copies:
+    for copy in factors:
         copy.start()
 
-    step = 32
-    for which, gain in ((0, pol_gain), (1, ref_gain)):
-        first[which].wait()
-
-        def norm(i, carry, which=which, gain=gain):
-            at = pl.ds(pl.multiple_of(i * step, step), step)
-            v = hid[which, at, :].astype(f32)
-            ms = jnp.sum(v * v, axis=-1, keepdims=True) * (1.0 / WIDTH)
-            n = (v * lax.rsqrt(ms + NORM_EPS) * gain[...]).astype(bf16)
-            for k in range(Y):
-                normed[k, pl.ds(pl.multiple_of(which * ROWS + i * step, step), step), :] = n[:, k * KY : (k + 1) * KY]
-            return carry
-
-        lax.fori_loop(0, ROWS // step, norm, 0)
-
-
-    def order(q):
-        return jnp.where(q == 2, 3, jnp.where(q == 3, 2, q))
-
-    for half in range(2):
-        core = c if half == 0 else 1 - c
-        for i in range(4):
-            copies[half * 4 + i].wait()
-
-        def column(s, carry, half=half, core=core):
-            xq = lax.rem(x + X - order(s), X)
-            j = core * X + xq
-            at = pl.ds(pl.multiple_of(xq * 16, 16), 16)
-            ysn, blk = [], []
-            for n in range(4):
-                ysn.append(lax.rem(y + Y - SHIFTS[n], Y))
-                blk.append((half * 4 + jnp.where(core == 0, n, s), jnp.where(core == 0, s, n)))
-            total = None
-            for n in range(4):
-                part = bdot(normed[ysn[n]], held[blk[n][0], blk[n][1], 0:KY, :], ((1,), (0,)))
-                total = part if total is None else total + part
-            acc[j] = total
-
-            for n in range(4):
-                ys = ysn[n]
-                e = held[blk[n][0], blk[n][1], KY:PIECE, :]
-
-                @pl.when(core == 0)
-                def _(ys=ys, e=e):
-                    for z in range(ZH):
-                        up[ys, at, z * TM : (z + 1) * TM] = e[z * 16 : (z + 1) * 16, 0:TM]
-
-                @pl.when(core == 1)
-                def _(ys=ys, e=e):
-                    down[ys, at, :] = jnp.concatenate(
-                        [e[z * 16 : (z + 1) * 16, 0:KM] for z in range(ZH)], axis=1
-                    )
-
-            return carry
-
-        lax.fori_loop(0, 4, column, 0)
+    rows.wait()
+    normalize(hid, ref_gain, normed, ROWS)
+
+    policy.wait()
+
+    def columns(s, carry):
+        core = jnp.where(s < X, c, 1 - c)
+        q = lax.rem(s, X)
+        shift = jnp.where(q == 2, SHIFTS[2], jnp.where(q == 3, SHIFTS[3], q))
+        j = core * X + lax.rem(x + X - shift, X)
+        pltpu.make_async_copy(held.at[j], held.at[j], sems.at[j]).wait()
+        for which in range(2):
+            at = slice(which * ROWS, (which + 1) * ROWS)
+            acc[j, at] = bdot(normed[at, :], held[j], ((1,), (0,)))
+        return carry
+
+    lax.fori_loop(0, C * X, columns, 0)
+
+    for copy in factors:
+        copy.wait()
+    for i in range(8):
+
+        @pl.when(place_of(i, 0)[0] == 0)
+        def _(i=i):
+            for q in range(4):
+                _, xq, ys = place_of(i, q)
+                at = pl.ds(pl.multiple_of(xq * 16, 16), 16)
+                for z in range(ZH):
+                    up[ys, at, z * TM : (z + 1) * TM] = extra[i, q, z * 16 : (z + 1) * 16, 0:TM]
+
+        @pl.when(place_of(i, 0)[0] == 1)
+        def _(i=i):
+            for q in range(4):
+                _, xq, ys = place_of(i, q)
+                at = pl.ds(pl.multiple_of(xq * 16, 16), 16)
+                down[ys, at, :] = jnp.concatenate(
+                    [extra[i, q, z * 16 : (z + 1) * 16, 0:KM] for z in range(ZH)], axis=1
+                )
 
     low = jnp.zeros((ROWS, RANK), f32)
     for k in range(Y):
-        low += bdot(normed[k, 0:ROWS], down[k], ((1,), (1,)))
+        low += bdot(normed[0:ROWS, k * KY : (k + 1) * KY], down[k], ((1,), (1,)))
     low16 = low.astype(bf16)
     low_t[...] = low.T.astype(bf16)
 
@@ -143,29 +183,29 @@
     def up_part(j):
         return up[j // 2, :, (j % 2) * NB : (j % 2 + 1) * NB]
 
-    s_pol = jnp.zeros((ROWS, 1), f32)
-    s_ref = jnp.zeros((ROWS, 1), f32)
-    hit = jnp.zeros((ROWS, 1), f32)
+    s_pol = jnp.zeros((ROWS, 128), f32)
+    s_ref = jnp.zeros((ROWS, 128), f32)
+    hit = jnp.zeros((ROWS, 128), f32)
     for j in range(8):
         v = acc[j, 0:ROWS] + bdot(low16, up_part(j), ((1,), (0,)))
         acc[j, 0:ROWS] = v
-        s_pol += jnp.sum(jnp.exp(v), axis=-1, keepdims=True)
-        hit += jnp.sum(jnp.where(iota == acts - j * NB, v, 0.0), axis=-1, keepdims=True)
-        s_ref += jnp.sum(jnp.exp(acc[j, ROWS:]), axis=-1, keepdims=True)
-    lse_pol, lse_ref = jnp.log(s_pol), jnp.log(s_ref)
-    taken = hit - lse_pol
+        s_pol += fold(jnp.exp(v))
+        hit += fold(jnp.where(iota == acts - j * NB, v, 0.0))
+        s_ref += fold(jnp.exp(acc[j, ROWS:]))
+    lse_pol, lse_ref = jnp.log(total_of(s_pol)), jnp.log(total_of(s_ref))
+    taken = total_of(hit) - lse_pol
     t = jnp.tanh((taken - old) / CLIP_LOG)
     pull = mask * (adv * jnp.exp(CLIP_LOG * t) * (1.0 - t * t))
-    div = jnp.zeros((ROWS, 1), f32)
+    div = jnp.zeros((ROWS, 128), f32)
     for j in range(8):
         logp = acc[j, 0:ROWS] - lse_pol
         gap = logp - (acc[j, ROWS:] - lse_ref).astype(bf16).astype(f32)
         p = jnp.exp(logp)
-        div += jnp.sum(p * gap, axis=-1, keepdims=True)
+        div += fold(p * gap)
         acc[j, 0:ROWS] = p
         acc[j, ROWS:] = gap
     scale = mask * KL_COEF
-    base = pull - scale * div
+    base = pull - scale * total_of(div)
     low_slopes = jnp.zeros((ROWS, RANK), f32)
     for j in range(8):
         s = acc[j, 0:ROWS] * (scale * acc[j, ROWS:] + base) - jnp.where(iota == acts - j * NB, pull, 0.0)
@@ -174,7 +214,7 @@
         low_slopes += bdot(s16, up_part(j), ((1,), (1,)))
     low_slopes_t = low_slopes.T.astype(bf16)
     for k in range(Y):
-        grad[:, TOKENS + k * KY : TOKENS + (k + 1) * KY] = bdot(low_slopes_t, normed[k, 0:ROWS], ((1,), (0,)))
+        grad[:, TOKENS + k * KY : TOKENS + (k + 1) * KY] = bdot(low_slopes_t, normed[0:ROWS, k * KY : (k + 1) * KY], ((1,), (0,)))
 
     blank = jnp.zeros((8, LANES - TM - KM), f32)
     for out, core in ((keep, c), (give, 1 - c)):
@@ -209,7 +249,9 @@
     own = [four] + [shift_second(four, k) for k in SHIFTS[1:]]
     other = [swap_cores(v) for v in own]
 
-    ref_hidden, guard = lax.optimization_barrier((ref_hidden, swap_cores(mine[:16, :NB])))
+    ref_hidden, guard, pol_hidden = lax.optimization_barrier(
+        (ref_hidden, swap_cores(mine[:16, :NB]), pol_hidden)
+    )
     ref_rows = lax.all_to_all(
         ref_hidden.reshape(Y * ZH, ROWS // (Y * ZH), WIDTH), ("y", "zh"), 0, 0, tiled=True
     ).reshape(ROWS, WIDTH)
@@ -223,30 +265,41 @@
 
     vmem = pl.BlockSpec(memory_space=pltpu.VMEM)
     hbm = pl.BlockSpec(memory_space=pl.ANY)
+    pol_normed = pl.pallas_call(
+        policy_kernel,
+        out_shape=jax.ShapeDtypeStruct((ROWS, WIDTH), bf16),
+        in_specs=[vmem, vmem],
+        out_specs=vmem,
+        compiler_params=pltpu.CompilerParams(vmem_limit_bytes=16 * 1024 * 1024),
+        cost_estimate=pl.CostEstimate(
+            flops=4 * ROWS * WIDTH, bytes_accessed=4 * ROWS * WIDTH, transcendentals=ROWS
+        ),
+    )(pol_rows, pol_gain.reshape(1, WIDTH))
     out = jax.ShapeDtypeStruct((X, Y * ZH, 8, LANES), f32)
     keep, give = pl.pallas_call(
         kernel,
         out_shape=(out, jax.ShapeDtypeStruct(out.shape, bf16)),
-        in_specs=[pl.BlockSpec(memory_space=pltpu.SMEM), hbm, hbm, vmem, vmem, vmem] + [hbm] * 8,
+        in_specs=[pl.BlockSpec(memory_space=pltpu.SMEM), hbm, hbm, vmem, vmem] + [hbm] * 8,
         out_specs=(vmem, vmem),
         scratch_shapes=[
-            pltpu.VMEM((8, 4, PIECE, NB), bf16),
-            pltpu.VMEM((Y, 2 * ROWS, KY), bf16),
+            pltpu.VMEM((C * X, WIDTH, NB), bf16),
+            pltpu.VMEM((8, 4, ZH * 16, NB), bf16),
+            pltpu.VMEM((2 * ROWS, WIDTH), bf16),
             pltpu.VMEM((C * X, 2 * ROWS, NB), f32),
             pltpu.VMEM((Y, RANK, TOKENS // Y), bf16),
             pltpu.VMEM((Y, RANK, KY), bf16),
             pltpu.VMEM((RANK, ROWS), bf16),
             pltpu.VMEM((RANK, TOKENS + WIDTH), f32),
-            pltpu.VMEM((2, ROWS, WIDTH), bf16),
+            pltpu.VMEM((ROWS, WIDTH), bf16),
             pltpu.SemaphoreType.DMA((10,)),
+            pltpu.SemaphoreType.DMA((8,)),
         ],
         compiler_params=pltpu.CompilerParams(vmem_limit_bytes=36 * 1024 * 1024),
         cost_estimate=pl.CostEstimate(
             flops=4 * ROWS * WIDTH * TOKENS, bytes_accessed=18 << 20, transcendentals=3 * ROWS * TOKENS
         ),
     )(
-        place, pol_rows, ref_rows,
-        pol_gain.reshape(1, WIDTH), ref_gain.reshape(1, WIDTH), rows8, *own, *other,
+        place, pol_normed, ref_rows, ref_gain.reshape(1, WIDTH), rows8, *own, *other,
     )
 
     part = (keep + swap_cores(give).astype(f32)).astype(bf16)

time: 211 us -> 209 us (level)
  waiting for transfers between devices: 40.1 us -> 37.2 us
  local copies, waits for them, and re-layouts: 4.59 us -> 7.12 us
    ppermute x6, waiting for transfers between devices: 5.31 us -> 2.14 us  [swap_cores(): return lax.ppermute(v, 'c', [(0, 1), (1, 0)])]
    unnamed x18 -> x22, local copies, waits for them, and re-layouts: 2.71 us -> 5.24 us
  transfers between devices with their start and end apart: 13 -> 13, of which waited for: 8 -> 6; matrix products, arithmetic and copies ran while one was open for 1% -> 1% of each run, Pallas kernels for 0% -> 0%
where the time goes in v3:
time: 209 us
  blocking collectives  85.8 us (41%)
  starting transfers between devices  59.8 us (29%)
  waiting for transfers between devices  37.2 us (18%)
  Pallas kernels  16.4 us (8%)
  local copies, waits for them, and re-layouts  7.12 us (3%)
    all_to_all x1, blocking collectives, local(): lax.all_to_all(jnp.broadcast_to(piece[None], (ZH, KM + 16, NB)), 'zh', 0,...  37.1 us
    ppermute x6, starting transfers between devices, swap_cores(): return lax.ppermute(v, 'c', [(0, 1), (1, 0)])  28.7 us
    all_to_all x1, blocking collectives, local(): lax.all_to_all(part, ('zl', 'zh'), 0, 0, tiled=True).astype(f32).sum(0)  25.8 us
    ppermute x3, waiting for transfers between devices, shift_second(): lax.ppermute(v, ('x', 'c', 'y'), pairs(lambda x, c, y: (x + k * (c == 1),...  23.3 us
    pallas_call x1, Pallas kernels, local(): pl.pallas_call(kernel, out_shape=(out, jax.ShapeDtypeStruct(out.shape, bf...  15.6 us
    all_to_all x1, blocking collectives, local(): lax.all_to_all(part.reshape(X * Y, ZH, 8, LANES), ('x', 'y'), 0, 0, tiled...  12.4 us
    ppermute x3, waiting for transfers between devices, shift_first(): lax.ppermute(v, ('x', 'c', 'y'), pairs(lambda x, c, y: (x + k * (c == 0),...  11.8 us
    all_to_all x1, starting transfers between devices, local(): lax.all_to_all(ref_hidden.reshape(Y * ZH, ROWS // (Y * ZH), WIDTH), ('y',...  11.1 us
  transfers between devices with their start and end apart: 13, of which 6 were waited for; matrix products, arithmetic and copies ran while one was open for 1% of the time, Pallas kernels for 0%

profile of v3, /device:TPU:1, one launch (start us, length us, event | category | flops | bytes accessed | tf_op | source)
XLA Modules:
  0.0 208.6 jit_solution(6173451525823934133)
XLA Ops:
  0.7 1.1 copy-done
  1.8 0.7 fusion
  2.6 37.1 %all_to_all.25 = bf16[4,208,256]{2,1,0:T(8,128)(2,1)S(1)} all-to-all(bf16[4,208,256]{2,1,0:T(8,128)(2,1)S(1)} %broadcast_in_dim.6), channel_id=1, replica_groups=mesh['x'=4,'zl'=4,'c'=2,'y'=4,'zh'=4] {'zh'}, dimensions={0} | all-to-all | bytes 851968 | tf_op jit(solution)/shard_map/all_to_all | solution.py:242
  39.7 3.7 %collective-permute-start = (bf16[16,256]{1,0:T(8,128)(2,1)S(1)}, bf16[16,256]{1,0:T(8,128)(2,1)S(1)}, u32[]{:S(2)}, u32[]{:S(2)}) collective-permute-start(bf16[16,256]{1,0:T(8,128)(2,1)S(1)} %slice.25), channel_id=1, source_target_pairs={{0,16},{16,0},{1,17},{17,1},{2,18},{18,2},{3,19},{19,3},{4,20},{20... | collective-permute-start | bytes 24584 | tf_op jit(solution)/shard_map/ppermute | solution.py:52
  43.5 0.8 collective-permute-done
  44.3 11.1 %all-to-all-start.1 = ((bf16[16,16,3072]{2,1,0:T(8,128)(2,1)}), bf16[16,16,3072]{2,1,0:T(8,128)(2,1)}, u32[]{:S(2)}, u32[]{:S(2)}) async-start(bf16[16,16,3072]{2,1,0:T(8,128)(2,1)} %bitcast.8), calls=%async_computation.1 | async-start | bytes 3145728 | tf_op jit(solution)/shard_map/all_to_all | solution.py:255
  55.5 4.4 %collective-permute-start.2 = (bf16[832,256]{1,0:T(8,128)(2,1)S(1)}, bf16[832,256]{1,0:T(8,128)(2,1)S(1)}, u32[]{:S(2)}, u32[]{:S(2)}) collective-permute-start(bf16[832,256]{1,0:T(8,128)(2,1)S(1)} %get-tuple-element.13), channel_id=1, source_target_pairs={{0,384},{4,388},{8,392},{12,396},{16,28},{20,16},{24,20},{28,24},{... | collective-permute-start | bytes 1277960 | tf_op jit(solution)/shard_map/ppermute | solution.py:44
  59.9 1.9 collective-permute-start.1
  61.8 3.7 %collective-permute-start.3 = (bf16[832,256]{1,0:T(8,128)(2,1)S(1)}, bf16[832,256]{1,0:T(8,128)(2,1)S(1)}, u32[]{:S(2)}, u32[]{:S(2)}) collective-permute-start(bf16[832,256]{1,0:T(8,128)(2,1)S(1)} %get-tuple-element.13), channel_id=1, source_target_pairs={{0,256},{4,260},{8,264},{12,268},{16,24},{20,28},{24,16},{28,20},{... | collective-permute-start | bytes 1277960 | tf_op jit(solution)/shard_map/ppermute | solution.py:44
  65.5 1.6 collective-permute-done.2
  67.1 10.2 %collective-permute-done.1 = bf16[832,256]{1,0:T(8,128)(2,1)S(1)} collective-permute-done((bf16[832,256]{1,0:T(8,128)(2,1)S(1)}, bf16[832,256]{1,0:T(8,128)(2,1)S(1)}, u32[]{:S(2)}, u32[]{:S(2)}) %collective-permute-start.1) | collective-permute-done | bytes 426016 | tf_op jit(solution)/shard_map/ppermute | solution.py:44
  77.6 4.7 %collective-permute-start.6 = (bf16[4,832,256]{2,1,0:T(8,128)(2,1)S(1)}, bf16[4,832,256]{2,1,0:T(8,128)(2,1)}, u32[]{:S(2)}, u32[]{:S(2)}) collective-permute-start(bf16[4,832,256]{2,1,0:T(8,128)(2,1)S(1)} %pad_maximum_fusion.p0), channel_id=1, source_target_pairs={{0,8},{4,12},{8,0},{12,4},{16,272},{20,276},{24,280},{28,284},{128... | collective-permute-start | bytes 5111816 | tf_op jit(solution)/shard_map/ppermute | solution.py:48
  82.2 2.8 %collective-permute-start.5 = (bf16[4,832,256]{2,1,0:T(8,128)(2,1)S(1)}, bf16[4,832,256]{2,1,0:T(8,128)(2,1)}, u32[]{:S(2)}, u32[]{:S(2)}) collective-permute-start(bf16[4,832,256]{2,1,0:T(8,128)(2,1)S(1)} %pad_maximum_fusion.p0), channel_id=1, source_target_pairs={{0,12},{4,0},{8,4},{12,8},{16,400},{20,404},{24,408},{28,412},{128... | collective-permute-start | bytes 5111816 | tf_op jit(solution)/shard_map/ppermute | solution.py:48
  85.0 2.5 %collective-permute-start.4 = (bf16[4,832,256]{2,1,0:T(8,128)(2,1)S(1)}, bf16[4,832,256]{2,1,0:T(8,128)(2,1)}, u32[]{:S(2)}, u32[]{:S(2)}) collective-permute-start(bf16[4,832,256]{2,1,0:T(8,128)(2,1)S(1)} %pad_maximum_fusion.p0), channel_id=1, source_target_pairs={{0,4},{4,8},{8,12},{12,0},{16,144},{20,148},{24,152},{28,156},{128... | collective-permute-start | bytes 5111816 | tf_op jit(solution)/shard_map/ppermute | solution.py:48
  87.5 2.4 %collective-permute-start.7 = (bf16[4,832,256]{2,1,0:T(8,128)(2,1)S(1)}, bf16[4,832,256]{2,1,0:T(8,128)(2,1)}, u32[]{:S(2)}, u32[]{:S(2)}) collective-permute-start(bf16[4,832,256]{2,1,0:T(8,128)(2,1)S(1)} %pad_maximum_fusion.p0), channel_id=1, source_target_pairs={{0,16},{16,0},{1,17},{17,1},{2,18},{18,2},{3,19},{19,3},{4,20},{20... | collective-permute-start | bytes 5111816 | tf_op jit(solution)/shard_map/ppermute | solution.py:52
  89.9 12.2 %collective-permute-done.6.p3 = bf16[4,832,256]{2,1,0:T(8,128)(2,1)} collective-permute-done((bf16[4,832,256]{2,1,0:T(8,128)(2,1)S(1)}, bf16[4,832,256]{2,1,0:T(8,128)(2,1)}, u32[]{:S(2)}, u32[]{:S(2)}) %collective-permute-start.6) | collective-permute-done | bytes 1703968 | tf_op jit(solution)/shard_map/ppermute | solution.py:48
  102.1 7.2 %collective-permute-start.10 = (bf16[4,832,256]{2,1,0:T(8,128)(2,1)}, bf16[4,832,256]{2,1,0:T(8,128)(2,1)}, u32[]{:S(2)}, u32[]{:S(2)}) collective-permute-start(bf16[4,832,256]{2,1,0:T(8,128)(2,1)} %collective-permute-done.6.p3), channel_id=1, source_target_pairs={{0,16},{16,0},{1,17},{17,1},{2,18},{18,2},{3,19},{19,3},{4,20},{20... | collective-permute-start | bytes 5111816 | tf_op jit(solution)/shard_map/ppermute | solution.py:52
  109.3 11.1 %collective-permute-done.5.p2 = bf16[4,832,256]{2,1,0:T(8,128)(2,1)} collective-permute-done((bf16[4,832,256]{2,1,0:T(8,128)(2,1)S(1)}, bf16[4,832,256]{2,1,0:T(8,128)(2,1)}, u32[]{:S(2)}, u32[]{:S(2)}) %collective-permute-start.5) | collective-permute-done | bytes 1703968 | tf_op jit(solution)/shard_map/ppermute | solution.py:48
  120.4 11.1 %collective-permute-start.9 = (bf16[4,832,256]{2,1,0:T(8,128)(2,1)}, bf16[4,832,256]{2,1,0:T(8,128)(2,1)}, u32[]{:S(2)}, u32[]{:S(2)}) collective-permute-start(bf16[4,832,256]{2,1,0:T(8,128)(2,1)} %collective-permute-done.5.p2), channel_id=1, source_target_pairs={{0,16},{16,0},{1,17},{17,1},{2,18},{18,2},{3,19},{19,3},{4,20},{20... | collective-permute-start | bytes 5111816 | tf_op jit(solution)/shard_map/ppermute | solution.py:52
  131.5 1.9 collective-permute-start.8
  134.3 1.4 copy-done.1
  135.7 0.8 shard_map.122.pol_hbm
  136.5 1.1 copy-done.2
  137.7 1.4 copy-done.3
  139.1 15.6 %shard_map.123 = (f32[4,16,8,384]{3,2,1,0:T(8,128)S(1)}, bf16[4,16,8,384]{3,2,1,0:T(8,128)(2,1)S(1)}) custom-call(s32[3]{0:T(128)S(1)} %pad_add_fusion.place, bf16[256,3072]{1,0:T(8,128)(2,1)S(1)} %copy-done.3, bf16[256,3072]{1,0:T(8,128)(2,1)} %bitcast.9.ref_hbm, f32[1,3072]{1,0:T(1,128)S(1)} %bitcast.26, f32[8,256]{1,0:T(8,128)S(1)} %stack.41.rows8, ...), custom_call_target="tpu_custom_call" | custom-call | flops 6442450944 | bytes 18874368 | tf_op jit(solution)/shard_map/pallas_call | solution.py:279
  154.7 2.4 %collective-permute-start.11 = (bf16[4,16,8,384]{3,2,1,0:T(8,128)(2,1)S(1)}, bf16[4,16,8,384]{3,2,1,0:T(8,128)(2,1)S(1)}, u32[]{:S(2)}, u32[]{:S(2)}) collective-permute-start(bf16[4,16,8,384]{3,2,1,0:T(8,128)(2,1)S(1)} %get-tuple-element.11), channel_id=1, source_target_pairs={{0,16},{16,0},{1,17},{17,1},{2,18},{18,2},{3,19},{19,3},{4,20},{20... | collective-permute-start | bytes 1179656 | tf_op jit(solution)/shard_map/ppermute | solution.py:52
  157.1 1.3 collective-permute-done.11
  158.6 12.4 %all_to_all.26 = bf16[16,4,8,384]{3,2,1,0:T(8,128)(2,1)S(1)} all-to-all(bf16[16,4,8,384]{3,2,1,0:T(8,128)(2,1)S(1)} %bitcast.29), channel_id=1, replica_groups=mesh['x'=4,'zl'=4,'c'=2,'y'=4,'zh'=4] {'x','y'}, dimensions={0} | all-to-all | bytes 786432 | tf_op jit(solution)/shard_map/all_to_all | solution.py:306
  171.0 25.8 %all_to_all.27 = bf16[16,8,384]{2,1,0:T(8,128)(2,1)S(1)} all-to-all(bf16[16,8,384]{2,1,0:T(8,128)(2,1)S(1)} %bitcast.35), channel_id=1, replica_groups=mesh['x'=4,'zl'=4,'c'=2,'y'=4,'zh'=4] {'zl','zh'}, dimensions={0} | all-to-all | bytes 196608 | tf_op jit(solution)/shard_map/all_to_all | solution.py:309
  196.9 10.5 %all_to_all.28 = f32[8,8,384]{2,1,0:T(8,128)S(1)} all-to-all(f32[8,8,384]{2,1,0:T(8,128)S(1)} %broadcast_in_dim.8), channel_id=1, replica_groups=mesh['x'=4,'zl'=4,'c'=2,'y'=4,'zh'=4] {'x','c'}, dimensions={0} | all-to-all | bytes 196608 | tf_op jit(solution)/shard_map/all_to_all | solution.py:310
  207.4 0.6 slice_bitcast_fusion.1
  208.0 0.6 slice_bitcast_fusion
  (51 shorter events, 1.4 us)
Async XLA Ops:
  0.6 1.1 copy-start
  39.7 4.6 %collective-permute-start = (bf16[16,256]{1,0:T(8,128)(2,1)S(1)}, bf16[16,256]{1,0:T(8,128)(2,1)S(1)}, u32[]{:S(2)}, u32[]{:S(2)}) collective-permute-start(bf16[16,256]{1,0:T(8,128)(2,1)S(1)} %slice.25), channel_id=1, source_target_pairs={{0,16},{16,0},{1,17},{17,1},{2,18},{18,2},{3,19},{19,3},{4,20},{20... | collective-permute-start | bytes 24584 | tf_op jit(solution)/shard_map/ppermute | solution.py:52
  44.3 93.4 %all-to-all-start.1 = ((bf16[16,16,3072]{2,1,0:T(8,128)(2,1)}), bf16[16,16,3072]{2,1,0:T(8,128)(2,1)}, u32[]{:S(2)}, u32[]{:S(2)}) async-start(bf16[16,16,3072]{2,1,0:T(8,128)(2,1)} %bitcast.8), calls=%async_computation.1 | async-start | bytes 3145728 | tf_op jit(solution)/shard_map/all_to_all | solution.py:255
  55.5 11.6 %collective-permute-start.2 = (bf16[832,256]{1,0:T(8,128)(2,1)S(1)}, bf16[832,256]{1,0:T(8,128)(2,1)S(1)}, u32[]{:S(2)}, u32[]{:S(2)}) collective-permute-start(bf16[832,256]{1,0:T(8,128)(2,1)S(1)} %get-tuple-element.13), channel_id=1, source_target_pairs={{0,384},{4,388},{8,392},{12,396},{16,28},{20,16},{24,20},{28,24},{... | collective-permute-start | bytes 1277960 | tf_op jit(solution)/shard_map/ppermute | solution.py:44
  59.9 17.4 %collective-permute-start.1 = (bf16[832,256]{1,0:T(8,128)(2,1)S(1)}, bf16[832,256]{1,0:T(8,128)(2,1)S(1)}, u32[]{:S(2)}, u32[]{:S(2)}) collective-permute-start(bf16[832,256]{1,0:T(8,128)(2,1)S(1)} %get-tuple-element.13), channel_id=1, source_target_pairs={{0,128},{4,132},{8,136},{12,140},{16,20},{20,24},{24,28},{28,16},{... | collective-permute-start | bytes 1277960 | tf_op jit(solution)/shard_map/ppermute | solution.py:44
  61.8 15.5 %collective-permute-start.3 = (bf16[832,256]{1,0:T(8,128)(2,1)S(1)}, bf16[832,256]{1,0:T(8,128)(2,1)S(1)}, u32[]{:S(2)}, u32[]{:S(2)}) collective-permute-start(bf16[832,256]{1,0:T(8,128)(2,1)S(1)} %get-tuple-element.13), channel_id=1, source_target_pairs={{0,256},{4,260},{8,264},{12,268},{16,24},{20,28},{24,16},{28,20},{... | collective-permute-start | bytes 1277960 | tf_op jit(solution)/shard_map/ppermute | solution.py:44
  77.3 56.1 %copy-start.8 = (s32[1,32,8]{1,2,0:T(8,128)S(1)}, s32[1,32,8]{1,2,0:T(8,128)}, u32[]{:S(2)}) copy-start(s32[1,32,8]{1,2,0:T(8,128)} %param.18) | copy-start | bytes 3076
  77.3 56.2 %copy-start.9 = (s32[1,32,8]{1,2,0:T(8,128)S(1)}, s32[1,32,8]{1,2,0:T(8,128)}, u32[]{:S(2)}) copy-start(s32[1,32,8]{1,2,0:T(8,128)} %param.19) | copy-start | bytes 3076
  77.3 56.5 %copy-start.6 = (f32[1,32,8]{1,2,0:T(8,128)S(1)}, f32[1,32,8]{1,2,0:T(8,128)}, u32[]{:S(2)}) copy-start(f32[1,32,8]{1,2,0:T(8,128)} %param.20) | copy-start | bytes 3076
  77.3 56.7 %copy-start.7 = (f32[1,32,8]{1,2,0:T(8,128)S(1)}, f32[1,32,8]{1,2,0:T(8,128)}, u32[]{:S(2)}) copy-start(f32[1,32,8]{1,2,0:T(8,128)} %param.21) | copy-start | bytes 3076
  77.3 57.0 %copy-start.4 = (f32[3072]{0:T(1024)S(1)}, f32[3072]{0:T(1024)}, u32[]{:S(2)}) copy-start(f32[3072]{0:T(1024)} %param.14) | copy-start | bytes 36868
  77.6 60.1 %copy-start.5 = (f32[3072]{0:T(1024)S(1)}, f32[3072]{0:T(1024)}, u32[]{:S(2)}) copy-start(f32[3072]{0:T(1024)} %param.13) | copy-start | bytes 36868
  77.6 24.5 %collective-permute-start.6 = (bf16[4,832,256]{2,1,0:T(8,128)(2,1)S(1)}, bf16[4,832,256]{2,1,0:T(8,128)(2,1)}, u32[]{:S(2)}, u32[]{:S(2)}) collective-permute-start(bf16[4,832,256]{2,1,0:T(8,128)(2,1)S(1)} %pad_maximum_fusion.p0), channel_id=1, source_target_pairs={{0,8},{4,12},{8,0},{12,4},{16,272},{20,276},{24,280},{28,284},{128... | collective-permute-start | bytes 5111816 | tf_op jit(solution)/shard_map/ppermute | solution.py:48
  82.2 38.2 %collective-permute-start.5 = (bf16[4,832,256]{2,1,0:T(8,128)(2,1)S(1)}, bf16[4,832,256]{2,1,0:T(8,128)(2,1)}, u32[]{:S(2)}, u32[]{:S(2)}) collective-permute-start(bf16[4,832,256]{2,1,0:T(8,128)(2,1)S(1)} %pad_maximum_fusion.p0), channel_id=1, source_target_pairs={{0,12},{4,0},{8,4},{12,8},{16,400},{20,404},{24,408},{28,412},{128... | collective-permute-start | bytes 5111816 | tf_op jit(solution)/shard_map/ppermute | solution.py:48
  85.0 46.5 %collective-permute-start.4 = (bf16[4,832,256]{2,1,0:T(8,128)(2,1)S(1)}, bf16[4,832,256]{2,1,0:T(8,128)(2,1)}, u32[]{:S(2)}, u32[]{:S(2)}) collective-permute-start(bf16[4,832,256]{2,1,0:T(8,128)(2,1)S(1)} %pad_maximum_fusion.p0), channel_id=1, source_target_pairs={{0,4},{4,8},{8,12},{12,0},{16,144},{20,148},{24,152},{28,156},{128... | collective-permute-start | bytes 5111816 | tf_op jit(solution)/shard_map/ppermute | solution.py:48
  87.5 50.1 %collective-permute-start.7 = (bf16[4,832,256]{2,1,0:T(8,128)(2,1)S(1)}, bf16[4,832,256]{2,1,0:T(8,128)(2,1)}, u32[]{:S(2)}, u32[]{:S(2)}) collective-permute-start(bf16[4,832,256]{2,1,0:T(8,128)(2,1)S(1)} %pad_maximum_fusion.p0), channel_id=1, source_target_pairs={{0,16},{16,0},{1,17},{17,1},{2,18},{18,2},{3,19},{19,3},{4,20},{20... | collective-permute-start | bytes 5111816 | tf_op jit(solution)/shard_map/ppermute | solution.py:52
  102.1 35.6 %collective-permute-start.10 = (bf16[4,832,256]{2,1,0:T(8,128)(2,1)}, bf16[4,832,256]{2,1,0:T(8,128)(2,1)}, u32[]{:S(2)}, u32[]{:S(2)}) collective-permute-start(bf16[4,832,256]{2,1,0:T(8,128)(2,1)} %collective-permute-done.6.p3), channel_id=1, source_target_pairs={{0,16},{16,0},{1,17},{17,1},{2,18},{18,2},{3,19},{19,3},{4,20},{20... | collective-permute-start | bytes 5111816 | tf_op jit(solution)/shard_map/ppermute | solution.py:52
  120.4 17.2 %collective-permute-start.9 = (bf16[4,832,256]{2,1,0:T(8,128)(2,1)}, bf16[4,832,256]{2,1,0:T(8,128)(2,1)}, u32[]{:S(2)}, u32[]{:S(2)}) collective-permute-start(bf16[4,832,256]{2,1,0:T(8,128)(2,1)} %collective-permute-done.5.p2), channel_id=1, source_target_pairs={{0,16},{16,0},{1,17},{17,1},{2,18},{18,2},{3,19},{19,3},{4,20},{20... | collective-permute-start | bytes 5111816 | tf_op jit(solution)/shard_map/ppermute | solution.py:52
  131.5 6.2 %collective-permute-start.8 = (bf16[4,832,256]{2,1,0:T(8,128)(2,1)}, bf16[4,832,256]{2,1,0:T(8,128)(2,1)}, u32[]{:S(2)}, u32[]{:S(2)}) collective-permute-start(bf16[4,832,256]{2,1,0:T(8,128)(2,1)} %collective-permute-done.4.p1), channel_id=1, source_target_pairs={{0,16},{16,0},{1,17},{17,1},{2,18},{18,2},{3,19},{19,3},{4,20},{20... | collective-permute-start | bytes 5111816 | tf_op jit(solution)/shard_map/ppermute | solution.py:52
  134.3 1.4 copy-start.1
  136.5 1.1 copy-start.2
  137.7 1.4 copy-start.3
  154.7 3.7 %collective-permute-start.11 = (bf16[4,16,8,384]{3,2,1,0:T(8,128)(2,1)S(1)}, bf16[4,16,8,384]{3,2,1,0:T(8,128)(2,1)S(1)}, u32[]{:S(2)}, u32[]{:S(2)}) collective-permute-start(bf16[4,16,8,384]{3,2,1,0:T(8,128)(2,1)S(1)} %get-tuple-element.11), channel_id=1, source_target_pairs={{0,16},{16,0},{1,17},{17,1},{2,18},{18,2},{3,19},{19,3},{4,20},{20... | collective-permute-start | bytes 1179656 | tf_op jit(solution)/shard_map/ppermute | solution.py:52

commit v4 on v3

--- a/solution.py
+++ b/solution.py
@@ -110,19 +110,6 @@
             sems.at[j],
         ).start()
 
-    for half in range(2):
-        for step in range(4):
-
-            @pl.when(place_of(half * 4, 0)[0] == 0)
-            def _(half=half, step=step):
-                for n in range(4):
-                    fetch(half * 4 + n, step)
-
-            @pl.when(place_of(half * 4, 0)[0] == 1)
-            def _(half=half, step=step):
-                for n in range(4):
-                    fetch(half * 4 + step, n)
-
     factors = [
         pltpu.make_async_copy(parts[i].at[:, pl.ds(KY, ZH * 16)], extra.at[i], extra_sems.at[i])
         for i in range(8)
@@ -130,23 +117,18 @@
     for copy in factors:
         copy.start()
 
-    rows.wait()
-    normalize(hid, ref_gain, normed, ROWS)
-
-    policy.wait()
-
-    def columns(s, carry):
-        core = jnp.where(s < X, c, 1 - c)
-        q = lax.rem(s, X)
-        shift = jnp.where(q == 2, SHIFTS[2], jnp.where(q == 3, SHIFTS[3], q))
-        j = core * X + lax.rem(x + X - shift, X)
-        pltpu.make_async_copy(held.at[j], held.at[j], sems.at[j]).wait()
-        for which in range(2):
-            at = slice(which * ROWS, (which + 1) * ROWS)
-            acc[j, at] = bdot(normed[at, :], held[j], ((1,), (0,)))
-        return carry
-
-    lax.fori_loop(0, C * X, columns, 0)
+    for half in range(2):
+        for step in range(4):
+
+            @pl.when(place_of(half * 4, 0)[0] == 0)
+            def _(half=half, step=step):
+                for n in range(4):
+                    fetch(half * 4 + n, step)
+
+            @pl.when(place_of(half * 4, 0)[0] == 1)
+            def _(half=half, step=step):
+                for n in range(4):
+                    fetch(half * 4 + step, n)
 
     for copy in factors:
         copy.wait()
@@ -169,11 +151,26 @@
                     [extra[i, q, z * 16 : (z + 1) * 16, 0:KM] for z in range(ZH)], axis=1
                 )
 
+    policy.wait()
     low = jnp.zeros((ROWS, RANK), f32)
     for k in range(Y):
         low += bdot(normed[0:ROWS, k * KY : (k + 1) * KY], down[k], ((1,), (1,)))
     low16 = low.astype(bf16)
     low_t[...] = low.T.astype(bf16)
+
+    rows.wait()
+    normalize(hid, ref_gain, normed, ROWS)
+
+    def columns(s, carry):
+        core = jnp.where(s < X, c, 1 - c)
+        q = lax.rem(s, X)
+        shift = jnp.where(q == 2, SHIFTS[2], jnp.where(q == 3, SHIFTS[3], q))
+        j = core * X + lax.rem(x + X - shift, X)
+        pltpu.make_async_copy(held.at[j], held.at[j], sems.at[j]).wait()
+        acc[j] = bdot(normed[...], held[j], ((1,), (0,)))
+        return carry
+
+    lax.fori_loop(0, C * X, columns, 0)
 
     cols = rows8[...].T
     acts = cols[:, 0:1].astype(jnp.int32)

time: 209 us -> 210 us (level)
  no operation moved by 1% of the time
where the time goes in v4:
time: 210 us; the launch traced here: 209 us
  blocking collectives  85.8 us (41%)
  starting transfers between devices  59.8 us (28%)
  waiting for transfers between devices  37.2 us (18%)
  Pallas kernels  16.5 us (8%)
  local copies, waits for them, and re-layouts  7.12 us (3%)
    all_to_all x1, blocking collectives, local(): lax.all_to_all(jnp.broadcast_to(piece[None], (ZH, KM + 16, NB)), 'zh', 0,...  37.1 us
    ppermute x6, starting transfers between devices, swap_cores(): return lax.ppermute(v, 'c', [(0, 1), (1, 0)])  28.7 us
    all_to_all x1, blocking collectives, local(): lax.all_to_all(part, ('zl', 'zh'), 0, 0, tiled=True).astype(f32).sum(0)  25.8 us
    ppermute x3, waiting for transfers between devices, shift_second(): lax.ppermute(v, ('x', 'c', 'y'), pairs(lambda x, c, y: (x + k * (c == 1),...  23.3 us
    pallas_call x1, Pallas kernels, local(): pl.pallas_call(kernel, out_shape=(out, jax.ShapeDtypeStruct(out.shape, bf...  15.7 us
    all_to_all x1, blocking collectives, local(): lax.all_to_all(part.reshape(X * Y, ZH, 8, LANES), ('x', 'y'), 0, 0, tiled...  12.4 us
    ppermute x3, waiting for transfers between devices, shift_first(): lax.ppermute(v, ('x', 'c', 'y'), pairs(lambda x, c, y: (x + k * (c == 0),...  11.8 us
    all_to_all x1, starting transfers between devices, local(): lax.all_to_all(ref_hidden.reshape(Y * ZH, ROWS // (Y * ZH), WIDTH), ('y',...  11.1 us
  transfers between devices with their start and end apart: 13, of which 6 were waited for; matrix products, arithmetic and copies ran while one was open for 1% of the time, Pallas kernels for 0%

profile of v4, /device:TPU:1, one launch (start us, length us, event | category | flops | bytes accessed | tf_op | source)
XLA Modules:
  0.0 208.7 jit_solution(3330191613000662548)
XLA Ops:
  0.7 1.1 copy-done
  1.8 0.7 fusion
  2.6 37.1 %all_to_all.25 = bf16[4,208,256]{2,1,0:T(8,128)(2,1)S(1)} all-to-all(bf16[4,208,256]{2,1,0:T(8,128)(2,1)S(1)} %broadcast_in_dim.6), channel_id=1, replica_groups=mesh['x'=4,'zl'=4,'c'=2,'y'=4,'zh'=4] {'zh'}, dimensions={0} | all-to-all | bytes 851968 | tf_op jit(solution)/shard_map/all_to_all | solution.py:239
  39.7 3.7 %collective-permute-start = (bf16[16,256]{1,0:T(8,128)(2,1)S(1)}, bf16[16,256]{1,0:T(8,128)(2,1)S(1)}, u32[]{:S(2)}, u32[]{:S(2)}) collective-permute-start(bf16[16,256]{1,0:T(8,128)(2,1)S(1)} %slice.25), channel_id=1, source_target_pairs={{0,16},{16,0},{1,17},{17,1},{2,18},{18,2},{3,19},{19,3},{4,20},{20... | collective-permute-start | bytes 24584 | tf_op jit(solution)/shard_map/ppermute | solution.py:52
  43.5 0.8 collective-permute-done
  44.3 11.1 %all-to-all-start.1 = ((bf16[16,16,3072]{2,1,0:T(8,128)(2,1)}), bf16[16,16,3072]{2,1,0:T(8,128)(2,1)}, u32[]{:S(2)}, u32[]{:S(2)}) async-start(bf16[16,16,3072]{2,1,0:T(8,128)(2,1)} %bitcast.8), calls=%async_computation.1 | async-start | bytes 3145728 | tf_op jit(solution)/shard_map/all_to_all | solution.py:252
  55.5 4.4 %collective-permute-start.2 = (bf16[832,256]{1,0:T(8,128)(2,1)S(1)}, bf16[832,256]{1,0:T(8,128)(2,1)S(1)}, u32[]{:S(2)}, u32[]{:S(2)}) collective-permute-start(bf16[832,256]{1,0:T(8,128)(2,1)S(1)} %get-tuple-element.13), channel_id=1, source_target_pairs={{0,384},{4,388},{8,392},{12,396},{16,28},{20,16},{24,20},{28,24},{... | collective-permute-start | bytes 1277960 | tf_op jit(solution)/shard_map/ppermute | solution.py:44
  59.9 1.9 collective-permute-start.1
  61.8 3.7 %collective-permute-start.3 = (bf16[832,256]{1,0:T(8,128)(2,1)S(1)}, bf16[832,256]{1,0:T(8,128)(2,1)S(1)}, u32[]{:S(2)}, u32[]{:S(2)}) collective-permute-start(bf16[832,256]{1,0:T(8,128)(2,1)S(1)} %get-tuple-element.13), channel_id=1, source_target_pairs={{0,256},{4,260},{8,264},{12,268},{16,24},{20,28},{24,16},{28,20},{... | collective-permute-start | bytes 1277960 | tf_op jit(solution)/shard_map/ppermute | solution.py:44
  65.5 1.6 collective-permute-done.2
  67.1 10.2 %collective-permute-done.1 = bf16[832,256]{1,0:T(8,128)(2,1)S(1)} collective-permute-done((bf16[832,256]{1,0:T(8,128)(2,1)S(1)}, bf16[832,256]{1,0:T(8,128)(2,1)S(1)}, u32[]{:S(2)}, u32[]{:S(2)}) %collective-permute-start.1) | collective-permute-done | bytes 426016 | tf_op jit(solution)/shard_map/ppermute | solution.py:44
  77.6 4.7 %collective-permute-start.6 = (bf16[4,832,256]{2,1,0:T(8,128)(2,1)S(1)}, bf16[4,832,256]{2,1,0:T(8,128)(2,1)}, u32[]{:S(2)}, u32[]{:S(2)}) collective-permute-start(bf16[4,832,256]{2,1,0:T(8,128)(2,1)S(1)} %pad_maximum_fusion.p0), channel_id=1, source_target_pairs={{0,8},{4,12},{8,0},{12,4},{16,272},{20,276},{24,280},{28,284},{128... | collective-permute-start | bytes 5111816 | tf_op jit(solution)/shard_map/ppermute | solution.py:48
  82.2 2.8 %collective-permute-start.5 = (bf16[4,832,256]{2,1,0:T(8,128)(2,1)S(1)}, bf16[4,832,256]{2,1,0:T(8,128)(2,1)}, u32[]{:S(2)}, u32[]{:S(2)}) collective-permute-start(bf16[4,832,256]{2,1,0:T(8,128)(2,1)S(1)} %pad_maximum_fusion.p0), channel_id=1, source_target_pairs={{0,12},{4,0},{8,4},{12,8},{16,400},{20,404},{24,408},{28,412},{128... | collective-permute-start | bytes 5111816 | tf_op jit(solution)/shard_map/ppermute | solution.py:48
  85.0 2.5 %collective-permute-start.4 = (bf16[4,832,256]{2,1,0:T(8,128)(2,1)S(1)}, bf16[4,832,256]{2,1,0:T(8,128)(2,1)}, u32[]{:S(2)}, u32[]{:S(2)}) collective-permute-start(bf16[4,832,256]{2,1,0:T(8,128)(2,1)S(1)} %pad_maximum_fusion.p0), channel_id=1, source_target_pairs={{0,4},{4,8},{8,12},{12,0},{16,144},{20,148},{24,152},{28,156},{128... | collective-permute-start | bytes 5111816 | tf_op jit(solution)/shard_map/ppermute | solution.py:48
  87.5 2.4 %collective-permute-start.7 = (bf16[4,832,256]{2,1,0:T(8,128)(2,1)S(1)}, bf16[4,832,256]{2,1,0:T(8,128)(2,1)}, u32[]{:S(2)}, u32[]{:S(2)}) collective-permute-start(bf16[4,832,256]{2,1,0:T(8,128)(2,1)S(1)} %pad_maximum_fusion.p0), channel_id=1, source_target_pairs={{0,16},{16,0},{1,17},{17,1},{2,18},{18,2},{3,19},{19,3},{4,20},{20... | collective-permute-start | bytes 5111816 | tf_op jit(solution)/shard_map/ppermute | solution.py:52
  89.9 12.2 %collective-permute-done.6.p3 = bf16[4,832,256]{2,1,0:T(8,128)(2,1)} collective-permute-done((bf16[4,832,256]{2,1,0:T(8,128)(2,1)S(1)}, bf16[4,832,256]{2,1,0:T(8,128)(2,1)}, u32[]{:S(2)}, u32[]{:S(2)}) %collective-permute-start.6) | collective-permute-done | bytes 1703968 | tf_op jit(solution)/shard_map/ppermute | solution.py:48
  102.1 7.2 %collective-permute-start.10 = (bf16[4,832,256]{2,1,0:T(8,128)(2,1)}, bf16[4,832,256]{2,1,0:T(8,128)(2,1)}, u32[]{:S(2)}, u32[]{:S(2)}) collective-permute-start(bf16[4,832,256]{2,1,0:T(8,128)(2,1)} %collective-permute-done.6.p3), channel_id=1, source_target_pairs={{0,16},{16,0},{1,17},{17,1},{2,18},{18,2},{3,19},{19,3},{4,20},{20... | collective-permute-start | bytes 5111816 | tf_op jit(solution)/shard_map/ppermute | solution.py:52
  109.3 11.1 %collective-permute-done.5.p2 = bf16[4,832,256]{2,1,0:T(8,128)(2,1)} collective-permute-done((bf16[4,832,256]{2,1,0:T(8,128)(2,1)S(1)}, bf16[4,832,256]{2,1,0:T(8,128)(2,1)}, u32[]{:S(2)}, u32[]{:S(2)}) %collective-permute-start.5) | collective-permute-done | bytes 1703968 | tf_op jit(solution)/shard_map/ppermute | solution.py:48
  120.4 11.1 %collective-permute-start.9 = (bf16[4,832,256]{2,1,0:T(8,128)(2,1)}, bf16[4,832,256]{2,1,0:T(8,128)(2,1)}, u32[]{:S(2)}, u32[]{:S(2)}) collective-permute-start(bf16[4,832,256]{2,1,0:T(8,128)(2,1)} %collective-permute-done.5.p2), channel_id=1, source_target_pairs={{0,16},{16,0},{1,17},{17,1},{2,18},{18,2},{3,19},{19,3},{4,20},{20... | collective-permute-start | bytes 5111816 | tf_op jit(solution)/shard_map/ppermute | solution.py:52
  131.5 1.9 collective-permute-start.8
  134.3 1.4 copy-done.1
  135.7 0.8 shard_map.122.pol_hbm
  136.5 1.1 copy-done.2
  137.7 1.4 copy-done.3
  139.1 15.7 %shard_map.123 = (f32[4,16,8,384]{3,2,1,0:T(8,128)S(1)}, bf16[4,16,8,384]{3,2,1,0:T(8,128)(2,1)S(1)}) custom-call(s32[3]{0:T(128)S(1)} %pad_add_fusion.place, bf16[256,3072]{1,0:T(8,128)(2,1)S(1)} %copy-done.3, bf16[256,3072]{1,0:T(8,128)(2,1)} %bitcast.9.ref_hbm, f32[1,3072]{1,0:T(1,128)S(1)} %bitcast.26, f32[8,256]{1,0:T(8,128)S(1)} %stack.41.rows8, ...), custom_call_target="tpu_custom_call" | custom-call | flops 6442450944 | bytes 18874368 | tf_op jit(solution)/shard_map/pallas_call | solution.py:276
  154.8 2.4 %collective-permute-start.11 = (bf16[4,16,8,384]{3,2,1,0:T(8,128)(2,1)S(1)}, bf16[4,16,8,384]{3,2,1,0:T(8,128)(2,1)S(1)}, u32[]{:S(2)}, u32[]{:S(2)}) collective-permute-start(bf16[4,16,8,384]{3,2,1,0:T(8,128)(2,1)S(1)} %get-tuple-element.11), channel_id=1, source_target_pairs={{0,16},{16,0},{1,17},{17,1},{2,18},{18,2},{3,19},{19,3},{4,20},{20... | collective-permute-start | bytes 1179656 | tf_op jit(solution)/shard_map/ppermute | solution.py:52
  157.3 1.3 collective-permute-done.11
  158.7 12.4 %all_to_all.26 = bf16[16,4,8,384]{3,2,1,0:T(8,128)(2,1)S(1)} all-to-all(bf16[16,4,8,384]{3,2,1,0:T(8,128)(2,1)S(1)} %bitcast.29), channel_id=1, replica_groups=mesh['x'=4,'zl'=4,'c'=2,'y'=4,'zh'=4] {'x','y'}, dimensions={0} | all-to-all | bytes 786432 | tf_op jit(solution)/shard_map/all_to_all | solution.py:303
  171.1 25.8 %all_to_all.27 = bf16[16,8,384]{2,1,0:T(8,128)(2,1)S(1)} all-to-all(bf16[16,8,384]{2,1,0:T(8,128)(2,1)S(1)} %bitcast.35), channel_id=1, replica_groups=mesh['x'=4,'zl'=4,'c'=2,'y'=4,'zh'=4] {'zl','zh'}, dimensions={0} | all-to-all | bytes 196608 | tf_op jit(solution)/shard_map/all_to_all | solution.py:306
  197.0 10.5 %all_to_all.28 = f32[8,8,384]{2,1,0:T(8,128)S(1)} all-to-all(f32[8,8,384]{2,1,0:T(8,128)S(1)} %broadcast_in_dim.8), channel_id=1, replica_groups=mesh['x'=4,'zl'=4,'c'=2,'y'=4,'zh'=4] {'x','c'}, dimensions={0} | all-to-all | bytes 196608 | tf_op jit(solution)/shard_map/all_to_all | solution.py:307
  207.5 0.6 slice_bitcast_fusion.1
  208.1 0.6 slice_bitcast_fusion
  (51 shorter events, 1.4 us)
Async XLA Ops:
  0.6 1.1 copy-start
  39.7 4.6 %collective-permute-start = (bf16[16,256]{1,0:T(8,128)(2,1)S(1)}, bf16[16,256]{1,0:T(8,128)(2,1)S(1)}, u32[]{:S(2)}, u32[]{:S(2)}) collective-permute-start(bf16[16,256]{1,0:T(8,128)(2,1)S(1)} %slice.25), channel_id=1, source_target_pairs={{0,16},{16,0},{1,17},{17,1},{2,18},{18,2},{3,19},{19,3},{4,20},{20... | collective-permute-start | bytes 24584 | tf_op jit(solution)/shard_map/ppermute | solution.py:52
  44.3 93.4 %all-to-all-start.1 = ((bf16[16,16,3072]{2,1,0:T(8,128)(2,1)}), bf16[16,16,3072]{2,1,0:T(8,128)(2,1)}, u32[]{:S(2)}, u32[]{:S(2)}) async-start(bf16[16,16,3072]{2,1,0:T(8,128)(2,1)} %bitcast.8), calls=%async_computation.1 | async-start | bytes 3145728 | tf_op jit(solution)/shard_map/all_to_all | solution.py:252
  55.5 11.6 %collective-permute-start.2 = (bf16[832,256]{1,0:T(8,128)(2,1)S(1)}, bf16[832,256]{1,0:T(8,128)(2,1)S(1)}, u32[]{:S(2)}, u32[]{:S(2)}) collective-permute-start(bf16[832,256]{1,0:T(8,128)(2,1)S(1)} %get-tuple-element.13), channel_id=1, source_target_pairs={{0,384},{4,388},{8,392},{12,396},{16,28},{20,16},{24,20},{28,24},{... | collective-permute-start | bytes 1277960 | tf_op jit(solution)/shard_map/ppermute | solution.py:44
  59.9 17.4 %collective-permute-start.1 = (bf16[832,256]{1,0:T(8,128)(2,1)S(1)}, bf16[832,256]{1,0:T(8,128)(2,1)S(1)}, u32[]{:S(2)}, u32[]{:S(2)}) collective-permute-start(bf16[832,256]{1,0:T(8,128)(2,1)S(1)} %get-tuple-element.13), channel_id=1, source_target_pairs={{0,128},{4,132},{8,136},{12,140},{16,20},{20,24},{24,28},{28,16},{... | collective-permute-start | bytes 1277960 | tf_op jit(solution)/shard_map/ppermute | solution.py:44
  61.8 15.5 %collective-permute-start.3 = (bf16[832,256]{1,0:T(8,128)(2,1)S(1)}, bf16[832,256]{1,0:T(8,128)(2,1)S(1)}, u32[]{:S(2)}, u32[]{:S(2)}) collective-permute-start(bf16[832,256]{1,0:T(8,128)(2,1)S(1)} %get-tuple-element.13), channel_id=1, source_target_pairs={{0,256},{4,260},{8,264},{12,268},{16,24},{20,28},{24,16},{28,20},{... | collective-permute-start | bytes 1277960 | tf_op jit(solution)/shard_map/ppermute | solution.py:44
  77.3 56.1 %copy-start.8 = (s32[1,32,8]{1,2,0:T(8,128)S(1)}, s32[1,32,8]{1,2,0:T(8,128)}, u32[]{:S(2)}) copy-start(s32[1,32,8]{1,2,0:T(8,128)} %param.18) | copy-start | bytes 3076
  77.3 56.2 %copy-start.9 = (s32[1,32,8]{1,2,0:T(8,128)S(1)}, s32[1,32,8]{1,2,0:T(8,128)}, u32[]{:S(2)}) copy-start(s32[1,32,8]{1,2,0:T(8,128)} %param.19) | copy-start | bytes 3076
  77.3 56.5 %copy-start.6 = (f32[1,32,8]{1,2,0:T(8,128)S(1)}, f32[1,32,8]{1,2,0:T(8,128)}, u32[]{:S(2)}) copy-start(f32[1,32,8]{1,2,0:T(8,128)} %param.20) | copy-start | bytes 3076
  77.3 56.7 %copy-start.7 = (f32[1,32,8]{1,2,0:T(8,128)S(1)}, f32[1,32,8]{1,2,0:T(8,128)}, u32[]{:S(2)}) copy-start(f32[1,32,8]{1,2,0:T(8,128)} %param.21) | copy-start | bytes 3076
  77.3 57.0 %copy-start.4 = (f32[3072]{0:T(1024)S(1)}, f32[3072]{0:T(1024)}, u32[]{:S(2)}) copy-start(f32[3072]{0:T(1024)} %param.14) | copy-start | bytes 36868
  77.6 60.1 %copy-start.5 = (f32[3072]{0:T(1024)S(1)}, f32[3072]{0:T(1024)}, u32[]{:S(2)}) copy-start(f32[3072]{0:T(1024)} %param.13) | copy-start | bytes 36868
  77.6 24.5 %collective-permute-start.6 = (bf16[4,832,256]{2,1,0:T(8,128)(2,1)S(1)}, bf16[4,832,256]{2,1,0:T(8,128)(2,1)}, u32[]{:S(2)}, u32[]{:S(2)}) collective-permute-start(bf16[4,832,256]{2,1,0:T(8,128)(2,1)S(1)} %pad_maximum_fusion.p0), channel_id=1, source_target_pairs={{0,8},{4,12},{8,0},{12,4},{16,272},{20,276},{24,280},{28,284},{128... | collective-permute-start | bytes 5111816 | tf_op jit(solution)/shard_map/ppermute | solution.py:48
  82.2 38.2 %collective-permute-start.5 = (bf16[4,832,256]{2,1,0:T(8,128)(2,1)S(1)}, bf16[4,832,256]{2,1,0:T(8,128)(2,1)}, u32[]{:S(2)}, u32[]{:S(2)}) collective-permute-start(bf16[4,832,256]{2,1,0:T(8,128)(2,1)S(1)} %pad_maximum_fusion.p0), channel_id=1, source_target_pairs={{0,12},{4,0},{8,4},{12,8},{16,400},{20,404},{24,408},{28,412},{128... | collective-permute-start | bytes 5111816 | tf_op jit(solution)/shard_map/ppermute | solution.py:48
  85.0 46.5 %collective-permute-start.4 = (bf16[4,832,256]{2,1,0:T(8,128)(2,1)S(1)}, bf16[4,832,256]{2,1,0:T(8,128)(2,1)}, u32[]{:S(2)}, u32[]{:S(2)}) collective-permute-start(bf16[4,832,256]{2,1,0:T(8,128)(2,1)S(1)} %pad_maximum_fusion.p0), channel_id=1, source_target_pairs={{0,4},{4,8},{8,12},{12,0},{16,144},{20,148},{24,152},{28,156},{128... | collective-permute-start | bytes 5111816 | tf_op jit(solution)/shard_map/ppermute | solution.py:48
  87.5 50.1 %collective-permute-start.7 = (bf16[4,832,256]{2,1,0:T(8,128)(2,1)S(1)}, bf16[4,832,256]{2,1,0:T(8,128)(2,1)}, u32[]{:S(2)}, u32[]{:S(2)}) collective-permute-start(bf16[4,832,256]{2,1,0:T(8,128)(2,1)S(1)} %pad_maximum_fusion.p0), channel_id=1, source_target_pairs={{0,16},{16,0},{1,17},{17,1},{2,18},{18,2},{3,19},{19,3},{4,20},{20... | collective-permute-start | bytes 5111816 | tf_op jit(solution)/shard_map/ppermute | solution.py:52
  102.1 35.6 %collective-permute-start.10 = (bf16[4,832,256]{2,1,0:T(8,128)(2,1)}, bf16[4,832,256]{2,1,0:T(8,128)(2,1)}, u32[]{:S(2)}, u32[]{:S(2)}) collective-permute-start(bf16[4,832,256]{2,1,0:T(8,128)(2,1)} %collective-permute-done.6.p3), channel_id=1, source_target_pairs={{0,16},{16,0},{1,17},{17,1},{2,18},{18,2},{3,19},{19,3},{4,20},{20... | collective-permute-start | bytes 5111816 | tf_op jit(solution)/shard_map/ppermute | solution.py:52
  120.4 17.2 %collective-permute-start.9 = (bf16[4,832,256]{2,1,0:T(8,128)(2,1)}, bf16[4,832,256]{2,1,0:T(8,128)(2,1)}, u32[]{:S(2)}, u32[]{:S(2)}) collective-permute-start(bf16[4,832,256]{2,1,0:T(8,128)(2,1)} %collective-permute-done.5.p2), channel_id=1, source_target_pairs={{0,16},{16,0},{1,17},{17,1},{2,18},{18,2},{3,19},{19,3},{4,20},{20... | collective-permute-start | bytes 5111816 | tf_op jit(solution)/shard_map/ppermute | solution.py:52
  131.5 6.2 %collective-permute-start.8 = (bf16[4,832,256]{2,1,0:T(8,128)(2,1)}, bf16[4,832,256]{2,1,0:T(8,128)(2,1)}, u32[]{:S(2)}, u32[]{:S(2)}) collective-permute-start(bf16[4,832,256]{2,1,0:T(8,128)(2,1)} %collective-permute-done.4.p1), channel_id=1, source_target_pairs={{0,16},{16,0},{1,17},{17,1},{2,18},{18,2},{3,19},{19,3},{4,20},{20... | collective-permute-start | bytes 5111816 | tf_op jit(solution)/shard_map/ppermute | solution.py:52
  134.3 1.4 copy-start.1
  136.5 1.1 copy-start.2
  137.7 1.4 copy-start.3
  154.8 3.7 %collective-permute-start.11 = (bf16[4,16,8,384]{3,2,1,0:T(8,128)(2,1)S(1)}, bf16[4,16,8,384]{3,2,1,0:T(8,128)(2,1)S(1)}, u32[]{:S(2)}, u32[]{:S(2)}) collective-permute-start(bf16[4,16,8,384]{3,2,1,0:T(8,128)(2,1)S(1)} %get-tuple-element.11), channel_id=1, source_target_pairs={{0,16},{16,0},{1,17},{17,1},{2,18},{18,2},{3,19},{19,3},{4,20},{20... | collective-permute-start | bytes 1179656 | tf_op jit(solution)/shard_map/ppermute | solution.py:52
